TPU v7x, 32 devices: a whole 2x2x4 slice. The times are simulated.
32 devices in a mesh: page: 16 (over z, y, core), blk: 2 (over x).
Axes of the slice: x: 2, y: 2, z: 4, core: 2. Of those that a mesh axis runs over, the one named last changes fastest.
Arguments:
- tokens: bfloat16 [16, 720, 768], P('page', 'blk'), may hold values from -6 to 6
- patch_count: int32 [16], P('page'), may hold values from 49 to 196, as said below
- reading_rank: int32 [16, 720], P('page'), may hold values from 0 to 719, as said below
- boxes: int32 [2, 16, 720], P(None, 'page'), may hold values from 0 to 255
- text_kernel: float32 [9, 768], replicated, may hold values from -2 to 2
- patch_kernel: float32 [9, 768], replicated, may hold values from -2 to 2
- qkv_weight: bfloat16 [768, 2304], replicated, may hold values from -0.21875 to 0.21875
- rank_table: bfloat16 [12, 32], replicated, may hold values from -3 to 3
- box_tables: bfloat16 [2, 12, 64], replicated, may hold values from -3 to 3
- out_weight: bfloat16 [768, 768], replicated, may hold values from -0.4375 to 0.4375
- norm_gains: float32 [2, 768], replicated, may hold values from 0.5 to 1.5
- norm_shifts: float32 [2, 768], replicated, may hold values from -2 to 2
- up_weight: bfloat16 [768, 3072], replicated, may hold values from -0.21875 to 0.21875
- up_bias: float32 [3072], replicated, may hold values from -3 to 3
- down_weight: bfloat16 [3072, 768], replicated, may hold values from -0.15625 to 0.15625
- down_bias: float32 [768], replicated, may hold values from -3 to 3
- cotangent: bfloat16 [16, 720, 768], P('page', 'blk'), may hold values from -6 to 6
Outputs:
- layer_output: bfloat16 [16, 720, 768], P('page', 'blk')
- token_grad: float32 [16, 720, 768], P('page', 'blk')
- text_kernel_grad: float32 [9, 768], P(None, ('page', 'blk'))
- patch_kernel_grad: float32 [9, 768], P(None, ('page', 'blk'))
- qkv_weight_grad: float32 [768, 2304], P(('page', 'blk'))
- rank_table_grad: float32 [12, 32], replicated
- box_tables_grad: float32 [2, 12, 64], replicated
- out_weight_grad: float32 [768, 768], P(('page', 'blk'))
- norm_gains_grad: float32 [2, 768], P(None, ('page', 'blk'))
- norm_shifts_grad: float32 [2, 768], P(None, ('page', 'blk'))
- up_weight_grad: float32 [768, 3072], P(('page', 'blk'))
- up_bias_grad: float32 [3072], P(('page', 'blk'))
- down_weight_grad: float32 [3072, 768], P(('page', 'blk'))
- down_bias_grad: float32 [768], P(('page', 'blk'))
Inputs may be any that keep to these rules, and one draw needn't show every extreme that they name: `patch_count`: each page image has 49 or 196 patches; both counts occur in every draw. `reading_rank`: for each page, the first 512 entries are a permutation of 0 to 511 made of runs of 16 consecutive slots holding consecutive values in order, the runs permuted; patch slot s holds 512 + s.
All inputs are finite; a program needn't handle non-finite values.
Results may differ from a plain program's by a relative error of at most 0.015.
The roundings to bfloat16 on the way count: a program that leaves them out, or rounds other values in their place, can miss the bound.
Values may be sent and summed in bfloat16 or wider, within the bound.
No kernel may reach another device: no remote copies, remote signals or barrier semaphores. Data moves between devices by JAX's collectives and lax.ppermute only.
A program may use at most 256 MiB of HBM per device.

v0:
```python
import jax
import jax.numpy as jnp
from jax import lax
from jax.sharding import PartitionSpec as P

TEXT = 512
GRID_LO = 7
GRID_HI = 14
HEADS = 12
HEAD_DIM = 64
NB1 = 32
NB2 = 64


rank_marks = (1, 2, 3, 4, 5, 6, 7, 8, 12, 16, 23, 32, 46, 64, 91)
box_marks = tuple(range(1, 17)) + (19, 23, 27, 32, 39, 46, 54, 64, 77, 91, 108, 128, 153, 182, 216)
neg_fill = -1000000000.0
norm_eps = 1e-05
root_half = 0.7071067811865476
inv_root_tau = 0.3989422804014327
tap_list = ((1, -1), (1, 0), (1, 1), (2, -1), (2, 0), (2, 1), (3, -1), (3, 0), (3, 1))
cell_list = ((-1, -1), (-1, 0), (-1, 1), (0, -1), (0, 0), (0, 1), (1, -1), (1, 0), (1, 1))


def padded_2(block, sides, width):
    for axis, dim in sides:
        count = lax.axis_size(axis)
        forward = [(i, i + 1) for i in range(count - 1)]
        backward = [(target, source) for source, target in forward]
        low = lax.ppermute(
            lax.slice_in_dim(block, block.shape[dim] - width, None, axis=dim), axis, forward
        )
        high = lax.ppermute(lax.slice_in_dim(block, 0, width, axis=dim), axis, backward)
        block = jnp.concatenate([low, block, high], axis=dim)
    return block


def bucket(delta, marks, half):
    spread = jnp.abs(delta)
    counted = jnp.zeros(delta.shape, jnp.int32)
    for mark in marks:
        counted = counted + (spread >= mark).astype(jnp.int32)
    return counted + half * (delta > 0).astype(jnp.int32)


def gelu(values):
    return 0.5 * values * (1.0 + lax.erf(values * root_half))


def gelu_slope(values):
    return (
        0.5 * (1.0 + lax.erf(values * root_half))
        + values * jnp.exp(-0.5 * values * values) * inv_root_tau
    )


def layer_norm(values, gain, shift):
    center = values - jnp.mean(values, axis=-1, keepdims=True)
    inverse = lax.rsqrt(jnp.mean(center * center, axis=-1, keepdims=True) + norm_eps)
    normed = center * inverse
    return (normed * gain + shift, normed, inverse)


def norm_back(upstream, normed, inverse, gain):
    scaled = upstream * gain
    return inverse * (
        scaled
        - jnp.mean(scaled, axis=-1, keepdims=True)
        - normed * jnp.mean(scaled * normed, axis=-1, keepdims=True)
    )


def contract_rows(left, right):
    return lax.dot_general(
        left, right, (((0,), (0,)), ((), ())), preferred_element_type=jnp.float32
    )


def contract_cols(left, right):
    return lax.dot_general(
        left, right, (((1,), (1,)), ((), ())), preferred_element_type=jnp.float32
    )


def one_hot_rows(bucket_ids, bins):
    picks = bucket_ids[None] == jnp.arange(bins, dtype=jnp.int32)[:, None, None]
    return picks.astype(jnp.bfloat16).reshape(bins, -1)


def table_bias(table, bucket_ids, bins):
    spread = jnp.dot(table, one_hot_rows(bucket_ids, bins), preferred_element_type=jnp.float32)
    return spread.reshape((table.shape[0],) + bucket_ids.shape)


def table_grad(score_grad, bucket_ids, bins):
    flat = score_grad.reshape(score_grad.shape[0], -1)
    return contract_cols(flat, one_hot_rows(bucket_ids, bins))


def text_valid(places, offset):
    target = places + offset
    return (places >= 0) & (places < TEXT) & (target >= 0) & (target < TEXT)


def patch_cells(places, count):
    grid = jnp.where(count == GRID_HI * GRID_HI, GRID_HI, GRID_LO).astype(jnp.int32)
    slot = places - TEXT
    alive = (slot >= 0) & (slot < grid * grid)
    row_of = slot // grid
    column = slot % grid
    cells = []
    for number, (down, across) in enumerate(cell_list):
        valid = (
            alive
            & (row_of + down >= 0)
            & (row_of + down < grid)
            & (column + across >= 0)
            & (column + across < grid)
        )
        cells.append((number, down * grid + across, valid))
    return cells


def run_forward(local_tokens, count, ranks, box_x, box_y, weights):
    (
        text_kernel,
        patch_kernel,
        qkv_weight,
        rank_table,
        box_tables,
        out_weight,
        norm_gains,
        norm_shifts,
        up_weight,
        up_bias,
        down_weight,
        down_bias,
    ) = weights
    local_rows, width = local_tokens.shape
    seq_len = ranks.shape[0]
    first = lax.axis_index("blk") * local_rows
    places = first + jnp.arange(local_rows, dtype=jnp.int32)
    rimmed = padded_2(local_tokens, (("blk", 0),), 3).astype(jnp.float32)
    inputs = rimmed[3 : 3 + local_rows]
    mixed = inputs
    for number, (reach, side) in enumerate(tap_list):
        offset = reach * side
        valid = text_valid(places, offset)
        mixed = (
            mixed
            + jnp.where(valid[:, None], rimmed[3 + offset : 3 + offset + local_rows], 0.0)
            * text_kernel[number]
        )
    margin = GRID_HI + 1
    padded = jnp.pad(inputs, ((margin, margin), (0, 0)))
    for number, shift, valid in patch_cells(places, count):
        moved = lax.dynamic_slice_in_dim(padded, margin + shift, local_rows, 0)
        mixed = mixed + jnp.where(valid[:, None], moved, 0.0) * patch_kernel[number]
    mixed_low = mixed.astype(jnp.bfloat16)
    packed = jnp.dot(mixed_low, qkv_weight, preferred_element_type=jnp.float32).astype(jnp.bfloat16)
    queries = packed[:, :width]
    all_keys, all_values = (
        lax.all_gather(packed[:, width : 2 * width], "blk", axis=0, tiled=True),
        lax.all_gather(packed[:, 2 * width :], "blk", axis=0, tiled=True),
    )
    query_rank = lax.dynamic_slice_in_dim(ranks, first, local_rows)
    query_x = lax.dynamic_slice_in_dim(box_x, first, local_rows)
    query_y = lax.dynamic_slice_in_dim(box_y, first, local_rows)
    rank_ids = bucket(ranks[None, :] - query_rank[:, None], rank_marks, NB1 // 2)
    xbox_ids = bucket(box_x[None, :] - query_x[:, None], box_marks, NB2 // 2)
    ybox_ids = bucket(box_y[None, :] - query_y[:, None], box_marks, NB2 // 2)
    scale = HEAD_DIM ** (-0.5)
    dotted = (
        jnp.einsum(
            "qhd,khd->hqk",
            queries.reshape(local_rows, HEADS, HEAD_DIM),
            all_keys.reshape(seq_len, HEADS, HEAD_DIM),
            preferred_element_type=jnp.float32,
        )
        * scale
    )
    biased = dotted + table_bias(rank_table, rank_ids, NB1)
    biased = (
        biased + table_bias(box_tables[0], xbox_ids, NB2) + table_bias(box_tables[1], ybox_ids, NB2)
    )
    key_alive = jnp.arange(seq_len, dtype=jnp.int32) < TEXT + count
    scores = jnp.where(key_alive[None, None, :], biased, neg_fill)
    powered = jnp.exp(scores - jnp.max(scores, axis=-1, keepdims=True))
    shares = powered / jnp.sum(powered, axis=-1, keepdims=True)
    shares_low = shares.astype(jnp.bfloat16)
    context = (
        jnp.einsum(
            "hqk,khd->qhd",
            shares_low,
            all_values.reshape(seq_len, HEADS, HEAD_DIM),
            preferred_element_type=jnp.float32,
        )
        .reshape(local_rows, width)
        .astype(jnp.bfloat16)
    )
    resid_one = mixed + jnp.dot(context, out_weight, preferred_element_type=jnp.float32)
    hidden_one, normed_one, inv_one = layer_norm(resid_one, norm_gains[0], norm_shifts[0])
    hidden_low = hidden_one.astype(jnp.bfloat16)
    pre_act = jnp.dot(hidden_low, up_weight, preferred_element_type=jnp.float32) + up_bias
    act_low = gelu(pre_act).astype(jnp.bfloat16)
    resid_two = (
        hidden_one + jnp.dot(act_low, down_weight, preferred_element_type=jnp.float32) + down_bias
    )
    result, normed_two, inv_two = layer_norm(resid_two, norm_gains[1], norm_shifts[1])
    row_alive = (places < TEXT + count).astype(jnp.float32)
    return {
        "places": places,
        "rimmed": rimmed,
        "mixed_low": mixed_low,
        "queries": queries,
        "all_keys": all_keys,
        "all_values": all_values,
        "rank_ids": rank_ids,
        "xbox_ids": xbox_ids,
        "ybox_ids": ybox_ids,
        "shares": shares,
        "shares_low": shares_low,
        "context": context,
        "normed_one": normed_one,
        "inv_one": inv_one,
        "hidden_low": hidden_low,
        "pre_act": pre_act,
        "act_low": act_low,
        "result": result,
        "normed_two": normed_two,
        "inv_two": inv_two,
        "row_alive": row_alive,
    }


def per_device(
    tokens,
    patch_count,
    reading_rank,
    boxes,
    text_kernel,
    patch_kernel,
    qkv_weight,
    rank_table,
    box_tables,
    out_weight,
    norm_gains,
    norm_shifts,
    up_weight,
    up_bias,
    down_weight,
    down_bias,
    cotangent,
):
    weights = (
        text_kernel,
        patch_kernel,
        qkv_weight,
        rank_table,
        box_tables,
        out_weight,
        norm_gains,
        norm_shifts,
        up_weight,
        up_bias,
        down_weight,
        down_bias,
    )
    count = patch_count[0]
    ranks = reading_rank[0]
    box_x = boxes[0, 0]
    box_y = boxes[1, 0]
    local_tokens = tokens[0]
    local_rows, width = local_tokens.shape
    seq_len = ranks.shape[0]
    scale = HEAD_DIM ** (-0.5)
    saved = run_forward(local_tokens, count, ranks, box_x, box_y, weights)
    layer_output = (saved["result"] * saved["row_alive"][:, None]).astype(jnp.bfloat16)
    out_grad = cotangent[0].astype(jnp.float32) * saved["row_alive"][:, None]
    gain_two = jnp.sum(out_grad * saved["normed_two"], axis=0)
    shift_two = jnp.sum(out_grad, axis=0)
    resid_two_grad = norm_back(out_grad, saved["normed_two"], saved["inv_two"], norm_gains[1])
    down_bias_grad = jnp.sum(resid_two_grad, axis=0)
    branch_grad = resid_two_grad.astype(jnp.bfloat16)
    down_weight_grad = contract_rows(saved["act_low"], branch_grad)
    pre_grad = (contract_cols(branch_grad, down_weight) * gelu_slope(saved["pre_act"])).astype(
        jnp.bfloat16
    )
    up_bias_grad = jnp.sum(pre_grad.astype(jnp.float32), axis=0)
    up_weight_grad = contract_rows(saved["hidden_low"], pre_grad)
    hidden_grad = resid_two_grad + contract_cols(pre_grad, up_weight)
    gain_one = jnp.sum(hidden_grad * saved["normed_one"], axis=0)
    shift_one = jnp.sum(hidden_grad, axis=0)
    resid_one_grad = norm_back(hidden_grad, saved["normed_one"], saved["inv_one"], norm_gains[0])
    attend_grad = resid_one_grad.astype(jnp.bfloat16)
    out_weight_grad = contract_rows(saved["context"], attend_grad)
    context_grad = contract_cols(attend_grad, out_weight).astype(jnp.bfloat16)
    heads_context = context_grad.reshape(local_rows, HEADS, HEAD_DIM)
    shares = saved["shares"]
    shares_low = saved["shares_low"]
    share_grad = jnp.einsum(
        "qhd,khd->hqk",
        heads_context,
        saved["all_values"].reshape(seq_len, HEADS, HEAD_DIM),
        preferred_element_type=jnp.float32,
    )
    score_grad = (
        shares * (share_grad - jnp.sum(shares * share_grad, axis=-1, keepdims=True))
    ).astype(jnp.bfloat16)
    rank_table_grad = table_grad(score_grad, saved["rank_ids"], NB1)
    box_tables_grad = jnp.stack(
        [
            table_grad(score_grad, saved["xbox_ids"], NB2),
            table_grad(score_grad, saved["ybox_ids"], NB2),
        ]
    )
    query_grad = (
        jnp.einsum(
            "hqk,khd->qhd",
            score_grad,
            saved["all_keys"].reshape(seq_len, HEADS, HEAD_DIM),
            preferred_element_type=jnp.float32,
        ).reshape(local_rows, width)
        * scale
    )
    heads_query = saved["queries"].reshape(local_rows, HEADS, HEAD_DIM)
    count_rows = local_rows * lax.axis_size("blk")
    key_part = (
        jnp.einsum(
            "hqk,qhd->khd", score_grad, heads_query, preferred_element_type=jnp.float32
        ).reshape(count_rows, width)
        * scale
    )
    value_part = jnp.einsum(
        "hqk,qhd->khd", shares_low, heads_context, preferred_element_type=jnp.float32
    ).reshape(count_rows, width)
    key_value_grad = lax.psum_scatter(
        jnp.concatenate([key_part, value_part], axis=1).astype(jnp.bfloat16),
        "blk",
        scatter_dimension=0,
        tiled=True,
    ).astype(jnp.float32)
    packed_grad = jnp.concatenate([query_grad, key_value_grad], axis=1).astype(jnp.bfloat16)
    qkv_weight_grad = contract_rows(saved["mixed_low"], packed_grad)
    mixed_grad = resid_one_grad + contract_cols(packed_grad, qkv_weight)
    places = saved["places"]
    rimmed = saved["rimmed"]
    rim_grad = padded_2(mixed_grad.astype(jnp.bfloat16), (("blk", 0),), 3).astype(mixed_grad.dtype)
    token_grad = mixed_grad
    text_rows = []
    for number, (reach, side) in enumerate(tap_list):
        offset = reach * side
        valid = text_valid(places, offset)
        text_rows.append(
            jnp.sum(
                jnp.where(
                    valid[:, None], mixed_grad * rimmed[3 + offset : 3 + offset + local_rows], 0.0
                ),
                axis=0,
            )
        )
        back_valid = text_valid(places - offset, offset)
        token_grad = (
            token_grad
            + jnp.where(back_valid[:, None], rim_grad[3 - offset : 3 - offset + local_rows], 0.0)
            * text_kernel[number]
        )
    text_kernel_grad = jnp.stack(text_rows)
    margin = GRID_HI + 1
    padded = jnp.pad(rimmed[3 : 3 + local_rows], ((margin, margin), (0, 0)))
    patch_rows = []
    for number, shift, valid in patch_cells(places, count):
        moved = lax.dynamic_slice_in_dim(padded, margin + shift, local_rows, 0)
        patch_rows.append(jnp.sum(jnp.where(valid[:, None], mixed_grad * moved, 0.0), axis=0))
        spread = jnp.pad(
            jnp.where(valid[:, None], mixed_grad, 0.0) * patch_kernel[number],
            ((margin, margin), (0, 0)),
        )
        token_grad = token_grad + lax.dynamic_slice_in_dim(spread, margin - shift, local_rows, 0)
    patch_kernel_grad = jnp.stack(patch_rows)
    gains_grad = jnp.stack([gain_one, gain_two])
    shifts_grad = jnp.stack([shift_one, shift_two])
    summed = (
        lax.psum_scatter(text_kernel_grad, ("page", "blk"), scatter_dimension=1, tiled=True),
        lax.psum_scatter(patch_kernel_grad, ("page", "blk"), scatter_dimension=1, tiled=True),
        lax.psum_scatter(qkv_weight_grad, ("page", "blk"), scatter_dimension=0, tiled=True),
        lax.psum_scatter(out_weight_grad, ("page", "blk"), scatter_dimension=0, tiled=True),
        lax.psum_scatter(gains_grad, ("page", "blk"), scatter_dimension=1, tiled=True),
        lax.psum_scatter(shifts_grad, ("page", "blk"), scatter_dimension=1, tiled=True),
        lax.psum_scatter(up_weight_grad, ("page", "blk"), scatter_dimension=0, tiled=True),
        lax.psum_scatter(up_bias_grad, ("page", "blk"), scatter_dimension=0, tiled=True),
        lax.psum_scatter(down_weight_grad, ("page", "blk"), scatter_dimension=0, tiled=True),
        lax.psum_scatter(down_bias_grad, ("page", "blk"), scatter_dimension=0, tiled=True),
    )
    tables = lax.psum((rank_table_grad, box_tables_grad), ("page", "blk"))
    return (
        layer_output[None],
        token_grad[None],
        summed[0],
        summed[1],
        summed[2],
        tables[0],
        tables[1],
        summed[3],
        summed[4],
        summed[5],
        summed[6],
        summed[7],
        summed[8],
        summed[9],
    )


def solution(mesh):
    in_specs = (
        P("page", "blk", None),
        P("page"),
        P("page", None),
        P(None, "page", None),
        P(),
        P(),
        P(),
        P(),
        P(),
        P(),
        P(),
        P(),
        P(),
        P(),
        P(),
        P(),
        P("page", "blk", None),
    )
    out_specs = (
        P("page", "blk", None),
        P("page", "blk", None),
        P(None, ("page", "blk")),
        P(None, ("page", "blk")),
        P(("page", "blk"), None),
        P(),
        P(),
        P(("page", "blk"), None),
        P(None, ("page", "blk")),
        P(None, ("page", "blk")),
        P(("page", "blk"), None),
        P(("page", "blk")),
        P(("page", "blk"), None),
        P(("page", "blk")),
    )
    return jax.shard_map(
        per_device, mesh=mesh, in_specs=in_specs, out_specs=out_specs, check_vma=False
    )
```

profile of v0, /device:TPU:0, one launch (start us, length us, event | category | flops | bytes accessed | tf_op | source)
XLA Modules:
  0.0 1066.2 jit_solution(4249468054258745818)
XLA Ops:
  10.0 6.0 collective-permute-start
  22.0 3.1 sub.195
  27.8 3.5 broadcast_reduce_fusion
  31.3 3.1 sub.198
  36.8 3.1 sub.188
  39.9 4.1 broadcast_reduce_fusion.1
  44.0 3.1 sub.191
  48.2 3.1 sub.182
  51.3 3.5 broadcast_reduce_fusion.2
  54.7 3.1 sub.184
  61.2 4.9 select_add_fusion.3
  66.0 12.3 %convolution_bitcast_fusion = f32[12,259200]{1,0:T(8,128)} fusion(s32[259200]{0:T(1024)S(1)} %select_add_fusion.3, bf16[1,12,64]{2,0,1:T(2,128)(2,1)S(1)} %copy-done.59), kind=kOutput, calls=%fused_computation.1 | convolution fusion | flops 414720000 | bytes 13479936 | tf_op jit(solution)/shard_map/dot_general | solution.py:91
  78.4 3.3 select_add_fusion.4
  81.8 12.7 %convolution_bitcast_fusion.1 = f32[12,259200]{1,0:T(8,128)} fusion(s32[259200]{0:T(1024)S(1)} %select_add_fusion.4, bf16[1,12,64]{2,0,1:T(2,128)(2,1)S(1)} %copy-done.58), kind=kOutput, calls=%fused_computation.2 | convolution fusion | flops 414720000 | bytes 13479936 | tf_op jit(solution)/shard_map/dot_general | solution.py:91
  96.2 8.7 convolution_bitcast_fusion.2
  106.9 22.7 %reshape.681 = f32[12,360,720]{2,1,0:T(8,128)} reshape(f32[12,259200]{1,0:T(8,128)} %convolution_bitcast_fusion) | data formatting | bytes 24883200 | tf_op jit(solution)/shard_map/reshape | solution.py:92
  129.6 22.9 %reshape.680 = f32[12,360,720]{2,1,0:T(8,128)} reshape(f32[12,259200]{1,0:T(8,128)} %convolution_bitcast_fusion.1) | data formatting | bytes 24883200 | tf_op jit(solution)/shard_map/reshape | solution.py:92
  152.5 23.1 %reshape.679 = f32[12,360,720]{2,1,0:T(8,128)} reshape(f32[12,259200]{1,0:T(8,128)} %convolution_bitcast_fusion.2) | data formatting | bytes 24883200 | tf_op jit(solution)/shard_map/reshape | solution.py:92
  178.1 4.1 multiply_add_fusion.1
  185.0 5.3 select_add_fusion
  190.3 4.6 select_add_fusion.1
  197.1 11.5 %all-gather.5.cloned.1.call-done = bf16[720,768]{1,0:T(8,128)(2,1)} async-done(((bf16[360,768]{1,0:T(8,128)(2,1)}), bf16[720,768]{1,0:T(8,128)(2,1)}) %all-gather.5.cloned.1.call-update) | async-done | bytes 1105936 | tf_op jit(solution)/shard_map/all_gather | solution.py:163
  211.1 21.3 %add_select_fusion = f32[12,360,720]{2,1,0:T(8,128)} fusion(f32[12,360,720]{2,1,0:T(8,128)} %reshape.681, f32[12,360,720]{2,1,0:T(8,128)} %reshape.680, f32[12,360,720]{2,1,0:T(8,128)} %reshape.679, bf16[360,12,64]{0,2,1:T(8,128)(2,1)} %bitcast.99, bf16[720,12,64]{0,2,1:T(8,128)(2,1)} %bitcast.96, pred[720]{0:T(1024)(128)(4,1)S(1)} %copy-done.104), kind=kOutput, calls=%fused_computation.22 | convolution fusion | flops 413683200 | bytes 51426000 | tf_op jit(solution)/shard_map/qhd,khd->hqk/dot_general | solution.py:174
  232.4 16.2 %fusion.211 = (f32[12,360]{1,0:T(8,128)}, f32[12,360,720]{2,1,0:T(8,128)}) fusion(f32[12,360,720]{2,1,0:T(8,128)} %add_select_fusion), kind=kOutput, calls=%fused_computation.411 | output fusion | flops 6221519 | bytes 24900480 | tf_op jit(solution)/shard_map/sub | solution.py:188
  251.0 17.7 %fusion.104 = bf16[12,64,360]{2,1,0:T(8,128)(2,1)} fusion(bf16[720,12,64]{0,2,1:T(8,128)(2,1)} %bitcast.105, f32[12,360]{1,0:T(8,128)} %get-tuple-element.154, f32[12,360,720]{2,1,0:T(8,128)} %add_select_fusion), kind=kOutput, calls=%fused_computation.133 | convolution fusion | flops 407743904 | bytes 14117760 | tf_op jit(solution)/shard_map/hqk,khd->qhd/dot_general | solution.py:192
  272.1 4.5 multiply_convert_fusion.1
  283.0 4.0 convert_reduce_fusion
  287.0 2.8 multiply_reduce_fusion.1
  294.8 18.0 %fusion.100 = bf16[12,64,720]{2,1,0:T(8,128)(2,1)} fusion(bf16[360,12,64]{0,2,1:T(8,128)(2,1)} %bitcast.108, f32[12,360]{1,0:T(8,128)} %get-tuple-element.154, f32[12,360,720]{2,1,0:T(8,128)} %add_select_fusion), kind=kOutput, calls=%fused_computation.129 | convolution fusion | flops 408020384 | bytes 14117760 | tf_op jit(solution)/shard_map/hqk,qhd->khd/dot_general | solution.py:334
  312.9 12.8 %multiply_reduce_fusion = (f32[12,360]{1,0:T(8,128)S(1)}, f32[12,360,720]{2,1,0:T(8,128)}) fusion(f32[12,360,720]{2,1,0:T(8,128)} %get-tuple-element.155, f32[12,360]{1,0:T(8,128)} %get-tuple-element.154, bf16[360,12,64]{0,2,1:T(8,128)(2,1)} %bitcast.109, bf16[720,12,64]{0,2,1:T(8,128)(2,1)} %bitcast.106), kind=kOutput, calls=%fused_computation.20 | convolution fusion | flops 407458080 | bytes 26576640 | tf_op jit(solution)/shard_map/qhd,khd->hqk/dot_general | solution.py:301
  325.7 6.3 multiply_convert_fusion
  336.5 4.3 copy.63
  348.1 16.8 %fusion.112 = f32[1,12,64]{2,1,0:T(8,128)S(1)} fusion(s32[360,720]{1,0:T(8,128)} %select_add_fusion, bf16[12,360,720]{2,1,0:T(8,128)(2,1)} %copy-done.3), kind=kOutput, calls=%fused_computation.149 | convolution fusion | flops 414720000 | bytes 7260672 | tf_op jit(solution)/shard_map/dot_general | solution.py:80
  364.9 12.1 %fusion.115 = f32[1,12,64]{2,1,0:T(8,128)S(1)} fusion(s32[360,720]{1,0:T(8,128)S(1)} %copy-done.23, bf16[12,360,720]{2,1,0:T(8,128)(2,1)S(1)} %bitcast.93), kind=kOutput, calls=%fused_computation.150 | convolution fusion | flops 414720000 | bytes 7260672 | tf_op jit(solution)/shard_map/dot_general | solution.py:80
  380.4 7.7 fusion.109
  390.6 7.6 select_reduce_fusion.7
  398.4 3.2 select_reduce_fusion
  417.7 3.6 fusion.158
  422.0 8.5 fusion.203
  430.8 8.3 fusion.161
  439.1 6.7 fusion.108
  449.5 5.7 collective-permute-start.2
  457.6 6.8 fusion.127
  464.4 78.0 %all-reduce.18.cloned.1.call-done = (f32[9,768]{1,0:T(8,128)}, f32[9,768]{1,0:T(8,128)}, f32[12,32]{1,0:T(8,128)}, f32[2,12,64]{2,1,0:T(8,128)}, f32[2,768]{1,0:...) async-done(((f32[9,768]{1,0:T(8,128)}, f32[9,768]{1,0:T(8,128)}, f32[12,32]{1,0:T(8,128)}, f32[2,12,64]{2,1,0:T(8,128)}, f32[2,768]{1,0:T(2,128)}, ...) | async-done | bytes 90640
  551.6 97.7 %reduce-scatter.14.cloned.1.call-done = f32[24,768]{1,0:T(8,128)} async-done(((f32[768,768]{1,0:T(8,128)}), f32[24,768]{1,0:T(8,128)}) %reduce-scatter.14.cloned.1.call-update) | async-done | bytes 73744 | tf_op jit(solution)/shard_map/reduce_scatter | solution.py:387
  649.3 141.7 %reduce-scatter.16.cloned.1.call-done = f32[24,3072]{1,0:T(8,128)} async-done(((f32[768,3072]{1,0:T(8,128)}), f32[24,3072]{1,0:T(8,128)}) %reduce-scatter.16.cloned.1.call-update) | async-done | bytes 294928 | tf_op jit(solution)/shard_map/reduce_scatter | solution.py:390
  790.9 141.3 %reduce-scatter.18.cloned.1.call-done = f32[96,768]{1,0:T(8,128)} async-done(((f32[3072,768]{1,0:T(8,128)}), f32[96,768]{1,0:T(8,128)}) %reduce-scatter.18.cloned.1.call-update) | async-done | bytes 294928 | tf_op jit(solution)/shard_map/reduce_scatter | solution.py:392
  932.3 125.4 %reduce-scatter.12.cloned.1.call-done = f32[24,2304]{1,0:T(8,128)} async-done(((f32[768,2304]{1,0:T(8,128)}), f32[24,2304]{1,0:T(8,128)}) %reduce-scatter.12.cloned.1.call-update) | async-done | bytes 221200 | tf_op jit(solution)/shard_map/reduce_scatter | solution.py:386
  (363 shorter events, 98.8 us)
Async XLA Ops:
  7.2 175.1 %copy-start = (bf16[768,2304]{1,0:T(8,128)(2,1)S(1)}, bf16[768,2304]{1,0:T(8,128)(2,1)}, u32[]{:S(2)}) copy-start(bf16[768,2304]{1,0:T(8,128)(2,1)} %param.23) | copy-start | bytes 10616836
  7.2 201.4 %all-gather.5.cloned.1.call-start = ((), (), s32[]{:S(2)}) async-start(), calls=%async_computation.6 | async-start | bytes 1658880 | tf_op jit(solution)/shard_map/all_gather | solution.py:163
  8.7 166.9 %collective-permute-start.1 = (bf16[3,768]{1,0:T(4,128)(2,1)}, bf16[3,768]{1,0:T(4,128)(2,1)}, u32[]{:S(2)}, u32[]{:S(2)}) collective-permute-start(bf16[3,768]{1,0:T(4,128)(2,1)} %get-tuple-element.141), channel_id=1, source_target_pairs={{1,0},{3,2},{5,4},{7,6},{9,8},{11,10},{13,12},{15,14},{17,16},{19,... | collective-permute-start | bytes 13832 | tf_op jit(solution)/shard_map/ppermute | solution.py:33
  10.0 165.6 %collective-permute-start = (bf16[3,768]{1,0:T(4,128)(2,1)}, bf16[3,768]{1,0:T(4,128)(2,1)}, u32[]{:S(2)}, u32[]{:S(2)}) collective-permute-start(bf16[3,768]{1,0:T(4,128)(2,1)} %get-tuple-element.140), channel_id=1, source_target_pairs={{0,1},{2,3},{4,5},{6,7},{8,9},{10,11},{12,13},{14,15},{16,17},{18,... | collective-permute-start | bytes 13832 | tf_op jit(solution)/shard_map/ppermute | solution.py:30
  25.1 22.0 %copy-start.26 = (s32[720]{0:T(1024)}, s32[720]{0:T(1024)S(1)}, u32[]{:S(2)}) copy-start(s32[720]{0:T(1024)S(1)} %reduce.18) | copy-start | bytes 8644
  25.9 25.4 %copy-start.54 = (s32[360]{0:T(512)}, s32[360]{0:T(512)S(1)}, u32[]{:S(2)}) copy-start(s32[360]{0:T(512)S(1)} %fusion.197) | copy-start | bytes 4324
  66.0 12.4 %copy-start.15 = (s32[259200]{0:T(1024)S(1)}, s32[259200]{0:T(1024)}, u32[]{:S(2)}) copy-start(s32[259200]{0:T(1024)} %sub.188) | copy-start | bytes 3110404
  66.0 12.4 %copy-start.18 = (s32[259200]{0:T(1024)S(1)}, s32[259200]{0:T(1024)}, u32[]{:S(2)}) copy-start(s32[259200]{0:T(1024)} %sub.191) | copy-start | bytes 3110404
  81.7 12.8 %copy-start.16 = (s32[259200]{0:T(1024)S(1)}, s32[259200]{0:T(1024)}, u32[]{:S(2)}) copy-start(s32[259200]{0:T(1024)} %sub.182) | copy-start | bytes 3110404
  81.7 12.8 %copy-start.17 = (s32[259200]{0:T(1024)S(1)}, s32[259200]{0:T(1024)}, u32[]{:S(2)}) copy-start(s32[259200]{0:T(1024)} %sub.184) | copy-start | bytes 3110404
  96.2 8.7 copy-start.72
  96.2 8.7 copy-start.73
  185.0 63.7 %all-gather.3.cloned.1.call-start = ((), (), s32[]{:S(2)}) async-start(), calls=%async_computation.5 | async-start | bytes 1658880 | tf_op jit(solution)/shard_map/all_gather | solution.py:164
  197.0 14.1 %copy-start.104 = (pred[720]{0:T(1024)(128)(4,1)S(1)}, pred[720]{0:T(1024)(128)(4,1)}, u32[]{:S(2)}) copy-start(pred[720]{0:T(1024)(128)(4,1)} %iota_compare_fusion.18) | copy-start | bytes 2164
  197.0 191.0 %reduce-scatter.20.cloned.1.call-start = ((), (), s32[]{:S(2)}) async-start(), calls=%async_computation.11 | async-start | bytes 3317760
  268.7 7.9 slice-start.6
  271.4 18.5 %copy-start.4 = (f32[360,768]{1,0:T(8,128)}, f32[360,768]{1,0:T(8,128)S(1)}, u32[]{:S(2)}) copy-start(f32[360,768]{1,0:T(8,128)S(1)} %get-tuple-element.157) | copy-start | bytes 3317764
  271.7 18.2 %copy-start.52 = (f32[360]{0:T(512)}, f32[360]{0:T(512)S(1)}, u32[]{:S(2)}) copy-start(f32[360]{0:T(512)S(1)} %add_rsqrt_fusion.1) | copy-start | bytes 4324
  279.8 7.1 slice-start.8
  312.8 12.8 %slice-start.2 = ((s8[13271040]{0:T(1024)(128)(4,1)}), s8[4194304]{0:T(1024)(128)(4,1)S(1)}, s32[]{:S(2)}) async-start(s8[13271040]{0:T(1024)(128)(4,1)} %bitcast.94), calls=%async_computation.15 | async-start | bytes 8388608
  312.8 12.8 %slice-start.3 = ((s8[13271040]{0:T(1024)(128)(4,1)}), s8[4194304]{0:T(1024)(128)(4,1)S(1)}, s32[]{:S(2)}) async-start(s8[13271040]{0:T(1024)(128)(4,1)} %bitcast.94), calls=%async_computation.16 | async-start | bytes 8388608
  312.8 12.8 %slice-start.4 = ((s8[13271040]{0:T(1024)(128)(4,1)}), s8[4194304]{0:T(1024)(128)(4,1)S(1)}, s32[]{:S(2)}) async-start(s8[13271040]{0:T(1024)(128)(4,1)} %bitcast.94), calls=%async_computation.17 | async-start | bytes 8388608
  312.8 12.8 %slice-start.5 = ((s8[13271040]{0:T(1024)(128)(4,1)}), s8[688128]{0:T(1024)(128)(4,1)S(1)}, s32[]{:S(2)}) async-start(s8[13271040]{0:T(1024)(128)(4,1)} %bitcast.94), calls=%async_computation.18 | async-start | bytes 1376256
  312.8 12.8 %copy-start.24 = (f32[12,360]{1,0:T(8,128)S(1)}, f32[12,360]{1,0:T(8,128)}, u32[]{:S(2)}) copy-start(f32[12,360]{1,0:T(8,128)} %get-tuple-element.154) | copy-start | bytes 51844
  340.7 201.6 %all-reduce.18.cloned.1.call-start = ((), (), s32[]{:S(2)}) async-start(), calls=%async_computation.12 | async-start | bytes 303104
  341.4 23.5 %slice-start = ((s8[6635520]{0:T(1024)(128)(4,1)}), s8[4194304]{0:T(1024)(128)(4,1)S(1)}, s32[]{:S(2)}) async-start(s8[6635520]{0:T(1024)(128)(4,1)} %bitcast.92), calls=%async_computation.13 | async-start | bytes 8388608
  348.0 16.8 %slice-start.1 = ((s8[6635520]{0:T(1024)(128)(4,1)}), s8[2441216]{0:T(1024)(128)(4,1)S(1)}, s32[]{:S(2)}) async-start(s8[6635520]{0:T(1024)(128)(4,1)} %bitcast.92), calls=%async_computation.14 | async-start | bytes 4882432
  348.1 16.8 %copy-start.23 = (s32[360,720]{1,0:T(8,128)S(1)}, s32[360,720]{1,0:T(8,128)}, u32[]{:S(2)}) copy-start(s32[360,720]{1,0:T(8,128)} %select_add_fusion.1) | copy-start | bytes 3110404
  364.9 12.8 %copy-start.5 = (bf16[720,768]{0,1:T(8,128)(2,1)S(1)}, bf16[720,768]{0,1:T(8,128)(2,1)}, u32[]{:S(2)}) copy-start(bf16[720,768]{0,1:T(8,128)(2,1)} %copy.55) | copy-start | bytes 3317764
  390.5 7.7 copy-start.8
  390.5 7.7 copy-start.29
  390.5 7.7 copy-start.31
  390.5 7.7 copy-start.78
  390.5 7.7 copy-start.80
  390.5 7.7 copy-start.82
  390.5 7.7 copy-start.84
  390.5 7.7 copy-start.86
  390.5 7.7 copy-start.88
  417.6 231.7 %reduce-scatter.14.cloned.1.call-start = ((), (), s32[]{:S(2)}) async-start(), calls=%async_computation.8 | async-start | bytes 2433024 | tf_op jit(solution)/shard_map/reduce_scatter | solution.py:387
  421.3 369.6 %reduce-scatter.16.cloned.1.call-start = ((), (), s32[]{:S(2)}) async-start(), calls=%async_computation.9 | async-start | bytes 9732096 | tf_op jit(solution)/shard_map/reduce_scatter | solution.py:390
  430.5 501.8 %reduce-scatter.18.cloned.1.call-start = ((), (), s32[]{:S(2)}) async-start(), calls=%async_computation.10 | async-start | bytes 9732096 | tf_op jit(solution)/shard_map/reduce_scatter | solution.py:392
  439.0 618.6 %reduce-scatter.12.cloned.1.call-start = ((), (), s32[]{:S(2)}) async-start(), calls=%async_computation.7 | async-start | bytes 7299072 | tf_op jit(solution)/shard_map/reduce_scatter | solution.py:386
  445.8 11.6 %copy-start.33 = (f32[768]{0:T(1024)S(1)}, f32[768]{0:T(1024)}, u32[]{:S(2)}) copy-start(f32[768]{0:T(1024)} %get-tuple-element.92) | copy-start | bytes 9220
  445.8 11.6 %copy-start.35 = (f32[768]{0:T(1024)S(1)}, f32[768]{0:T(1024)}, u32[]{:S(2)}) copy-start(f32[768]{0:T(1024)} %get-tuple-element.186) | copy-start | bytes 9220
  445.9 11.6 %copy-start.37 = (f32[768]{0:T(1024)S(1)}, f32[768]{0:T(1024)}, u32[]{:S(2)}) copy-start(f32[768]{0:T(1024)} %get-tuple-element.187) | copy-start | bytes 9220
  445.9 11.6 %copy-start.39 = (f32[768]{0:T(1024)S(1)}, f32[768]{0:T(1024)}, u32[]{:S(2)}) copy-start(f32[768]{0:T(1024)} %get-tuple-element.188) | copy-start | bytes 9220
  448.3 7.7 collective-permute-start.3
  449.5 6.7 collective-permute-start.2
  (87 other events, 162.9 us)
Sparse Core Ops, SparseCore 0:
  185.1 23.4 all-gather.4
  210.1 21.9 all-gather.2
  340.9 33.0 reduce-scatter.19
  417.8 124.5 all-reduce.17
  548.1 101.1 reduce-scatter.13
  656.6 134.2 reduce-scatter.15
  797.4 134.8 reduce-scatter.17
  939.5 118.1 reduce-scatter.11
where the time goes:
time: 1080 us; the launch traced here: 1070 us
  waiting for transfers between devices  596 us (55%)
  matrix products  198 us (18%)
  local copies, waits for them, and re-layouts  163 us (15%)
  other arithmetic  78 us (7%)
  between operations  16.9 us (2%)
  starting transfers between devices  14.9 us (1%)
    reduce_scatter x1, waiting for transfers between devices, per_device(): lax.psum_scatter(up_weight_grad, ('page', 'blk'), scatter_dimension=0, ti...  142 us
    reduce_scatter x1, waiting for transfers between devices, per_device(): lax.psum_scatter(down_weight_grad, ('page', 'blk'), scatter_dimension=0,...  141 us
    reduce_scatter x1, waiting for transfers between devices, per_device(): lax.psum_scatter(qkv_weight_grad, ('page', 'blk'), scatter_dimension=0, t...  125 us
    reduce_scatter x1, waiting for transfers between devices, per_device(): lax.psum_scatter(out_weight_grad, ('page', 'blk'), scatter_dimension=0, t...  97.7 us
    unnamed x10, waiting for transfers between devices  78.1 us
    reshape x3, local copies, waits for them, and re-layouts, table_bias(): return spread.reshape((table.shape[0],) + bucket_ids.shape)  68.7 us
    dot_general x7, matrix products, contract_cols(): lax.dot_general(left, right, (((1,), (1,)), ((), ())), preferred_element_...  52.5 us
    dot_general x3, matrix products, table_bias(): jnp.dot(table, one_hot_rows(bucket_ids, bins), preferred_element_type=jnp...  33.8 us
  transfers between devices with their start and end apart: 12, of which 7 were waited for; matrix products, arithmetic and copies ran while one was open for 29% of the time, Pallas kernels for 0%

commit v1 on v0

v1 whole, which is shorter than its diff:
```python
import functools

import jax
import jax.numpy as jnp
import numpy as np
from jax import lax
from jax.experimental import pallas as pl
from jax.experimental.pallas import tpu as pltpu
from jax.sharding import PartitionSpec as P

TEXT = 512
GRID_LO = 7
GRID_HI = 14
RUN = 16
HEADS = 12
HEAD_DIM = 64
NB1 = 32
NB2 = 64
SPAN = 256
RANK_LANES = 1536
RANK_MID = RANK_LANES // 2
ROWS = 128
F32 = jnp.float32
BF16 = jnp.bfloat16
MIB = 1 << 20

rank_marks = (1, 2, 3, 4, 5, 6, 7, 8, 12, 16, 23, 32, 46, 64, 91)
box_marks = tuple(range(1, 17)) + (19, 23, 27, 32, 39, 46, 54, 64, 77, 91, 108, 128, 153, 182, 216)
neg_fill = -1000000000.0
norm_eps = 1e-05
root_half = 0.7071067811865476
inv_root_tau = 0.3989422804014327
tap_list = ((1, -1), (1, 0), (1, 1), (2, -1), (2, 0), (2, 1), (3, -1), (3, 0), (3, 1))
cell_list = ((-1, -1), (-1, 0), (-1, 1), (0, -1), (0, 0), (0, 1), (1, -1), (1, 0), (1, 1))


def bucket_rows(deltas, marks, bins):
    spread = np.abs(deltas)
    ids = np.sum(spread[:, None] >= np.asarray(marks)[None, :], axis=1) + (bins // 2) * (deltas > 0)
    return (ids[:, None] == np.arange(bins)[None, :]).astype(np.float32)


def gelu(values):
    return 0.5 * values * (1.0 + lax.erf(values * root_half))


def gelu_slope(values):
    return (
        0.5 * (1.0 + lax.erf(values * root_half))
        + values * jnp.exp(-0.5 * values * values) * inv_root_tau
    )


def layer_norm(values, gain, shift):
    center = values - jnp.mean(values, axis=-1, keepdims=True)
    inverse = lax.rsqrt(jnp.mean(center * center, axis=-1, keepdims=True) + norm_eps)
    normed = center * inverse
    return (normed * gain + shift, normed, inverse)


def norm_back(upstream, normed, inverse, gain):
    scaled = upstream * gain
    return inverse * (
        scaled
        - jnp.mean(scaled, axis=-1, keepdims=True)
        - normed * jnp.mean(scaled * normed, axis=-1, keepdims=True)
    )


def dot_nn(left, right):
    return lax.dot_general(left, right, (((1,), (0,)), ((), ())), preferred_element_type=F32)


def dot_nt(left, right):
    return lax.dot_general(left, right, (((1,), (1,)), ((), ())), preferred_element_type=F32)


def dot_tn(left, right):
    return lax.dot_general(left, right, (((0,), (0,)), ((), ())), preferred_element_type=F32)


def row_chunks(total, size):
    return [(start, min(size, total - start)) for start in range(0, total, size)]


def vmem():
    return pl.BlockSpec(memory_space=pltpu.VMEM)


def smem():
    return pl.BlockSpec(memory_space=pltpu.SMEM)


def params(mib):
    return pltpu.CompilerParams(vmem_limit_bytes=mib * MIB)


def onehot_kernel(rank_ref, box_ref, xy_ref, xyt_ref):
    seq = rank_ref.shape[1]
    for start, size in row_chunks(seq, 240):
        spot = lax.broadcasted_iota(jnp.int32, (size, seq), 0) + start
        order = (spot == rank_ref[...]).astype(F32).astype(BF16)
        for half in range(2):
            level = lax.broadcasted_iota(jnp.int32, (SPAN, seq), 0)
            marks = (level == box_ref[half : half + 1, :]).astype(F32).astype(BF16)
            xy_ref[start : start + size, half * SPAN : (half + 1) * SPAN] = dot_nt(
                order, marks
            ).astype(BF16)
    row = lax.broadcasted_iota(jnp.int32, (SPAN, SPAN), 0)
    col = lax.broadcasted_iota(jnp.int32, (SPAN, SPAN), 1)
    flip = (row + col == SPAN - 1).astype(F32).astype(BF16)
    for half in range(2):
        part = slice(half * SPAN, (half + 1) * SPAN)
        xyt_ref[part, :] = dot_nt(flip, xy_ref[:, part]).astype(BF16)


def onehots(ranks, boxes):
    seq = ranks.shape[0]
    return pl.pallas_call(
        onehot_kernel,
        out_shape=(
            jax.ShapeDtypeStruct((seq, 2 * SPAN), BF16),
            jax.ShapeDtypeStruct((2 * SPAN, seq), BF16),
        ),
        in_specs=[vmem(), vmem()],
        out_specs=(vmem(), vmem()),
        compiler_params=params(32),
        cost_estimate=pl.CostEstimate(
            flops=4 * seq * seq * SPAN, bytes_accessed=4 * seq * 2 * SPAN, transcendentals=0
        ),
        name="onehots",
    )(ranks[None, :], boxes)


def place_slots(own_ref, other_ref, side, text, patch, patch_pad):
    local = own_ref.shape[0]
    head = TEXT - local
    groups = text.shape[0]

    def place(low_ref, high_ref):
        for lane in range(groups):
            cols = slice(128 * lane, 128 * lane + 128)
            text[lane, 8 : 8 + local, :] = low_ref[:, cols].astype(F32)
            high = high_ref[:, cols].astype(F32)
            text[lane, 8 + local : 8 + TEXT, :] = high[:head]
            patch[lane, patch_pad : patch_pad + local - head, :] = high[head:]

    pl.when(side == 0)(lambda: place(own_ref, other_ref))
    pl.when(side != 0)(lambda: place(other_ref, own_ref))


def clear_pads(text, patch, patch_pad):
    groups, rows = patch.shape[0], patch.shape[1]
    for lane in range(groups):
        text[lane, 0:8, :] = jnp.zeros((8, 128), F32)
        text[lane, 8 + TEXT : 16 + TEXT, :] = jnp.zeros((8, 128), F32)
        patch[lane, 0:patch_pad, :] = jnp.zeros((patch_pad, 128), F32)
        patch[lane, rows - patch_pad : rows, :] = jnp.zeros((patch_pad, 128), F32)


def cell_masks(grid, rows):
    slot = lax.broadcasted_iota(jnp.int32, (rows, 128), 0)
    row_of = jnp.zeros((rows, 128), jnp.int32)
    for line in range(1, grid):
        row_of = row_of + (slot >= line * grid).astype(jnp.int32)
    column = slot - row_of * grid
    alive = slot < grid * grid
    masks = []
    for down, across in cell_list:
        masks.append(
            alive
            & (row_of + down >= 0)
            & (row_of + down < grid)
            & (column + across >= 0)
            & (column + across < grid)
        )
    return masks


def store_masks(masks, fine, rows):
    for grid, chosen in ((GRID_HI, fine != 0), (GRID_LO, fine == 0)):

        def fill(grid=grid):
            for number, mask in enumerate(cell_masks(grid, rows)):
                masks[number] = mask.astype(F32)

        pl.when(chosen)(fill)


def mix_lane(text, patch, masks, out, lane, text_kernel, patch_kernel, fine, patch_pad, flip):
    cols = pl.ds(pl.multiple_of(lane * 128, 128), 128)
    taps = {}
    for number, (reach, side) in enumerate(tap_list):
        offset = -reach * side if flip else reach * side
        value = text_kernel[number : number + 1, cols]
        taps[offset] = taps[offset] + value if offset in taps else value
    for start, size in row_chunks(TEXT, ROWS):
        total = text[lane, pl.ds(8 + start, size), :] * (1.0 + taps[0])
        for offset, value in taps.items():
            if offset:
                total = total + text[lane, pl.ds(8 + start + offset, size), :] * value
        out[lane, pl.ds(start, size), :] = total
    rows = masks.shape[1]
    for grid, chosen in ((GRID_HI, fine != 0), (GRID_LO, fine == 0)):

        def cells(grid=grid):
            for start, size in row_chunks(rows, 104):
                total = patch[lane, pl.ds(patch_pad + start, size), :]
                for number, (down, across) in enumerate(cell_list):
                    tap = len(cell_list) - 1 - number if flip else number
                    moved = patch[lane, pl.ds(patch_pad + start + down * grid + across, size), :]
                    total = total + (
                        moved * masks[number, pl.ds(start, size), :]
                    ) * patch_kernel[tap : tap + 1, cols]
                out[lane, pl.ds(TEXT + start, size), :] = total

        pl.when(chosen)(cells)


def sort_rows(ranks_ref, source, target, seq, cast):
    for run in range(TEXT // RUN):
        spot = pl.multiple_of(ranks_ref[run * RUN], RUN)
        target[pl.ds(spot, RUN), :] = source[run * RUN : (run + 1) * RUN, :].astype(cast)
    target[TEXT:seq, :] = source[TEXT:seq, :].astype(cast)


def unsort_rows(ranks_ref, source, target, seq):
    for run in range(TEXT // RUN):
        spot = pl.multiple_of(ranks_ref[run * RUN], RUN)
        target[run * RUN : (run + 1) * RUN, :] = source[pl.ds(spot, RUN), :]
    target[TEXT:seq, :] = source[TEXT:seq, :]


def mix_kernel(
    scalars, ranks_ref, own_ref, other_ref, text_kernel, patch_kernel, weight_ref,
    mixed_ref, low_ref, packed_ref, text, patch, masks, lanes, whole,
):
    side, fine = scalars[0], scalars[2]
    local, width = own_ref.shape
    seq = low_ref.shape[0]
    groups = width // 128
    pad = GRID_HI + 2
    place_slots(own_ref, other_ref, side, text, patch, pad)
    clear_pads(text, patch, pad)
    store_masks(masks, fine, seq - TEXT)

    def one_lane(lane, carry):
        mix_lane(text, patch, masks, lanes, lane, text_kernel, patch_kernel, fine, pad, False)
        return carry

    lax.fori_loop(0, groups, one_lane, 0)
    for lane in range(groups):
        whole[:, 128 * lane : 128 * lane + 128] = lanes[lane]
    mixed_ref[...] = whole[pl.ds(pl.multiple_of(side * local, 8), local), :]
    sort_rows(ranks_ref, whole, low_ref, seq, BF16)
    part = width // 2
    for block in range(3):
        cols = pl.ds(pl.multiple_of(block * width + side * part, 128), part)
        weight = weight_ref[:, cols]
        for start, size in row_chunks(seq, 240):
            value = dot_nn(low_ref[start : start + size, :], weight).astype(BF16)
            if block == 0:
                value = value * (HEAD_DIM**-0.5)
            packed_ref[start : start + size, block * part : (block + 1) * part] = value


def mix_and_project(scalars, ranks, own, other, text_kernel, patch_kernel, qkv_weight):
    local, width = own.shape
    seq = ranks.shape[0]
    groups = width // 128
    return pl.pallas_call(
        mix_kernel,
        out_shape=(
            jax.ShapeDtypeStruct((local, width), F32),
            jax.ShapeDtypeStruct((seq, width), BF16),
            jax.ShapeDtypeStruct((seq, 3 * width // 2), BF16),
        ),
        in_specs=[smem(), smem()] + [vmem()] * 5,
        out_specs=(vmem(),) * 3,
        scratch_shapes=[
            pltpu.VMEM((groups, TEXT + 16, 128), F32),
            pltpu.VMEM((groups, seq - TEXT + 2 * (GRID_HI + 2), 128), F32),
            pltpu.VMEM((9, seq - TEXT, 128), F32),
            pltpu.VMEM((groups, seq, 128), F32),
            pltpu.VMEM((seq, width), F32),
        ],
        compiler_params=params(40),
        cost_estimate=pl.CostEstimate(
            flops=2 * seq * width * 3 * width // 2, bytes_accessed=12 * MIB, transcendentals=0
        ),
        name="mix_and_project",
    )(scalars, ranks, own, other, text_kernel, patch_kernel, qkv_weight)


def head_lanes(shape, parity):
    return (lax.broadcasted_iota(jnp.int32, shape, 1) >= HEAD_DIM) == (parity != 0)


def skewed(vector, rows, lanes, shift):
    return pltpu.roll(jnp.broadcast_to(vector, (rows, lanes)), shift, 1, stride=1, stride_axis=0)


def attend_kernel(
    scalars, ranks_ref, queries, keys, values, xy_ref, vectors,
    shares_ref, own_ref, other_ref, left, right, rank_bias, gathered, slots,
):
    side, live = scalars[0], scalars[1]
    seq = queries.shape[0]
    local = own_ref.shape[0]
    head = pl.program_id(0)
    parity = lax.rem(head, 2)

    @pl.when(head == 0)
    def _():
        left[:, 128:] = xy_ref[...]

    left[:, :128] = queries[...]
    mine = head_lanes((seq, 128), parity)
    right[:, :128] = jnp.where(mine, keys[...], jnp.zeros((), BF16))
    for half in range(2):
        table = skewed(vectors[0, half + 1 : half + 2, : 2 * SPAN], SPAN, 2 * SPAN, SPAN + 1)
        table = table[:, :SPAN].astype(BF16)
        right[:, 128 + half * SPAN : 128 + (half + 1) * SPAN] = dot_nn(
            xy_ref[:, half * SPAN : (half + 1) * SPAN], table
        ).astype(BF16)
    rank_bias[...] = skewed(vectors[0, 0:1, :], ROWS, RANK_LANES, RANK_LANES - 128)
    top = (seq // ROWS) * ROWS
    for start, size in row_chunks(seq, ROWS):
        scores = dot_nt(left[start : start + size, :], right[...])
        scores = scores + rank_bias[:size, top - start : top - start + seq]
        alive = lax.broadcasted_iota(jnp.int32, (size, seq), 1) < live
        scores = jnp.where(alive, scores, neg_fill)
        powered = jnp.exp(scores - jnp.max(scores, axis=1, keepdims=True))
        shares = powered * (1.0 / jnp.sum(powered, axis=1, keepdims=True))
        low = shares.astype(BF16)
        shares_ref[0, start : start + size, :] = low
        context = dot_nn(low, values[...])
        gathered[start : start + size, :] = jnp.where(
            head_lanes((size, 128), parity), context, gathered[start : start + size, :]
        )

    @pl.when(parity == 1)
    def _():
        unsort_rows(ranks_ref, gathered, slots, seq)
        own_ref[...] = slots[pl.ds(pl.multiple_of(side * local, 8), local), :].astype(BF16)
        other_ref[...] = slots[pl.ds(pl.multiple_of((1 - side) * local, 8), local), :].astype(BF16)


def attend(scalars, ranks, packed, xy, vectors, local):
    seq = packed.shape[0]
    heads = vectors.shape[0]
    pairs = heads // 2
    width = heads * HEAD_DIM
    whole = pl.BlockSpec((seq, 2 * SPAN), lambda h: (0, 0))
    slot_spec = pl.BlockSpec((local, 128), lambda h: (0, h // 2))
    return pl.pallas_call(
        attend_kernel,
        grid=(heads,),
        out_shape=(
            jax.ShapeDtypeStruct((heads, seq, seq), BF16),
            jax.ShapeDtypeStruct((local, width), BF16),
            jax.ShapeDtypeStruct((local, width), BF16),
        ),
        in_specs=[
            smem(),
            smem(),
            pl.BlockSpec((seq, 128), lambda h: (0, h // 2)),
            pl.BlockSpec((seq, 128), lambda h: (0, pairs + h // 2)),
            pl.BlockSpec((seq, 128), lambda h: (0, 2 * pairs + h // 2)),
            whole,
            pl.BlockSpec((1, 8, RANK_LANES), lambda h: (h, 0, 0)),
        ],
        out_specs=(pl.BlockSpec((1, seq, seq), lambda h: (h, 0, 0)), slot_spec, slot_spec),
        scratch_shapes=[
            pltpu.VMEM((seq, 128 + 2 * SPAN), BF16),
            pltpu.VMEM((seq, 128 + 2 * SPAN), BF16),
            pltpu.VMEM((ROWS, RANK_LANES), F32),
            pltpu.VMEM((seq, 128), F32),
            pltpu.VMEM((seq, 128), F32),
        ],
        compiler_params=params(40),
        cost_estimate=pl.CostEstimate(
            flops=heads * 2 * seq * seq * 1024,
            bytes_accessed=heads * seq * seq * 2,
            transcendentals=heads * seq * seq,
        ),
        name="attend",
    )(scalars, ranks, packed, packed, packed, xy, vectors)


def attend_back_kernel(
    ranks_ref, own_ref, other_ref, side_ref, shares_ref, queries, keys, values, xy_ref, xyt_ref,
    dq_ref, dk_ref, dv_ref, sums_ref, right, score_grad, spread, rank_sum, slots, upstream,
):
    seq = queries.shape[0]
    local = own_ref.shape[0]
    side = side_ref[0]
    head = pl.program_id(0)
    parity = lax.rem(head, 2)
    scale = HEAD_DIM**-0.5

    @pl.when(head == 0)
    def _():
        right[:, 128:] = xy_ref[...]

    @pl.when(parity == 0)
    def _():
        slots[pl.ds(pl.multiple_of(side * local, 8), local), :] = own_ref[...].astype(F32)
        slots[pl.ds(pl.multiple_of((1 - side) * local, 8), local), :] = other_ref[...].astype(F32)
        sort_rows(ranks_ref, slots, upstream, seq, BF16)

    right[:, :128] = keys[...]
    mine = head_lanes((seq, 128), parity)
    own_values = jnp.where(mine, values[...], jnp.zeros((), BF16))
    rank_sum[...] = jnp.zeros(rank_sum.shape, F32)
    top = (seq // ROWS) * ROWS
    for start, size in row_chunks(seq, ROWS):
        rows = slice(start, start + size)
        share_grad = dot_nt(upstream[rows, :], own_values)
        shares = shares_ref[0, rows, :].astype(F32)
        weighted = shares * share_grad
        low = (weighted - shares * jnp.sum(weighted, axis=1, keepdims=True)).astype(BF16)
        score_grad[rows, :] = low
        lanes = slice(top - start, top - start + seq)
        rank_sum[:size, lanes] = rank_sum[:size, lanes] + low.astype(F32)
        product = dot_nn(low, right[...])
        spread[rows, :] = product[:, 128:].astype(BF16)
        dq_ref[rows, :] = jnp.where(
            head_lanes((size, 128), parity), (product[:, :128] * scale).astype(BF16), dq_ref[rows, :]
        )
    dk = dot_tn(score_grad[...], queries[...]).astype(BF16)
    dk_ref[...] = jnp.where(mine, dk, dk_ref[...])
    dv = dot_tn(shares_ref[0], upstream[...]).astype(BF16)
    dv_ref[...] = jnp.where(mine, dv, dv_ref[...])
    row = lax.broadcasted_iota(jnp.int32, (ROWS, ROWS), 0)
    col = lax.broadcasted_iota(jnp.int32, (ROWS, ROWS), 1)
    flip = (row + col == ROWS - 1).astype(F32)
    turned = lax.dot_general(
        flip, rank_sum[...], (((1,), (0,)), ((), ())),
        precision=lax.Precision.HIGHEST, preferred_element_type=F32,
    )
    turned = pltpu.roll(turned, 0, 1, stride=1, stride_axis=0)
    sums_ref[0, 0:1, :] = jnp.sum(turned, axis=0, keepdims=True)
    for half in range(2):
        part = slice(half * SPAN, (half + 1) * SPAN)
        table = dot_nn(xyt_ref[part, :], spread[:, part])
        table = jnp.concatenate([table, jnp.zeros((SPAN, SPAN), F32)], axis=1)
        table = pltpu.roll(table, 0, 1, stride=1, stride_axis=0)
        sums_ref[0, half + 1 : half + 2, : 2 * SPAN] = jnp.sum(table, axis=0, keepdims=True)


def attend_back(scalars, ranks, own, other, shares, packed, xy, xyt):
    heads, seq, _ = shares.shape
    local = own.shape[0]
    pairs = heads // 2
    width = heads * HEAD_DIM
    slot_spec = pl.BlockSpec((local, 128), lambda h: (0, h // 2))
    out_spec = pl.BlockSpec((seq, 128), lambda h: (0, h // 2))
    return pl.pallas_call(
        attend_back_kernel,
        grid=(heads,),
        out_shape=(jax.ShapeDtypeStruct((seq, width), BF16),) * 3
        + (jax.ShapeDtypeStruct((heads, 8, RANK_LANES), F32),),
        in_specs=[
            smem(),
            slot_spec,
            slot_spec,
            smem(),
            pl.BlockSpec((1, seq, seq), lambda h: (h, 0, 0)),
            pl.BlockSpec((seq, 128), lambda h: (0, h // 2)),
            pl.BlockSpec((seq, 128), lambda h: (0, pairs + h // 2)),
            pl.BlockSpec((seq, 128), lambda h: (0, 2 * pairs + h // 2)),
            pl.BlockSpec((seq, 2 * SPAN), lambda h: (0, 0)),
            pl.BlockSpec((2 * SPAN, seq), lambda h: (0, 0)),
        ],
        out_specs=(out_spec,) * 3 + (pl.BlockSpec((1, 8, RANK_LANES), lambda h: (h, 0, 0)),),
        scratch_shapes=[
            pltpu.VMEM((seq, 128 + 2 * SPAN), BF16),
            pltpu.VMEM((seq, seq), BF16),
            pltpu.VMEM((seq, 2 * SPAN), BF16),
            pltpu.VMEM((ROWS, RANK_LANES), F32),
            pltpu.VMEM((seq, 128), F32),
            pltpu.VMEM((seq, 128), BF16),
        ],
        compiler_params=params(40),
        cost_estimate=pl.CostEstimate(
            flops=heads * 2 * seq * seq * 1600,
            bytes_accessed=heads * seq * seq * 2,
            transcendentals=0,
        ),
        name="attend_back",
    )(ranks, own, other, scalars, shares, packed, packed, packed, xy, xyt)


def project_back_kernel(order_ref, low_ref, dq_ref, dk_ref, dv_ref, keep_ref, send_ref):
    turned = dot_nt(order_ref[...], low_ref[...]).astype(BF16)
    half, part = keep_ref.shape[0], dq_ref.shape[1]
    for block, ref in enumerate((dq_ref, dk_ref, dv_ref)):
        cols = slice(block * part, (block + 1) * part)
        send_ref[:, cols] = dot_nn(turned[half:], ref[...]).astype(BF16)
        keep_ref[:, cols] = dot_nn(turned[:half], ref[...]).astype(BF16)


def project_weight_grad(order, low, dq, dk, dv):
    seq, width = low.shape
    shape = jax.ShapeDtypeStruct((width // 2, 3 * dq.shape[1]), BF16)
    return pl.pallas_call(
        project_back_kernel,
        out_shape=(shape, shape),
        in_specs=[vmem()] * 5,
        out_specs=(vmem(), vmem()),
        compiler_params=params(40),
        cost_estimate=pl.CostEstimate(
            flops=2 * seq * width * 5 * width // 2, bytes_accessed=8 * MIB, transcendentals=0
        ),
        name="project_weight_grad",
    )(order, low, dq, dk, dv)


def up_kernel(order_ref, hidden_ref, context_ref, grad_ref, attend_ref, keep_ref, send_ref, turned):
    step = pl.program_id(0)
    half = keep_ref.shape[0]
    last = pl.num_programs(0) - 1

    @pl.when(step == 0)
    def _():
        turned[...] = dot_nt(order_ref[...], hidden_ref[...]).astype(BF16)

    @pl.when(step == last)
    def _():
        turned[...] = dot_nt(order_ref[...], context_ref[...]).astype(BF16)

    def fill(right):
        send_ref[...] = dot_nn(turned[half:, :], right).astype(BF16)
        keep_ref[...] = dot_nn(turned[:half, :], right).astype(BF16)

    pl.when(step < last)(lambda: fill(grad_ref[...]))
    pl.when(step == last)(lambda: fill(attend_ref[...]))


def up_weight_grad(order, hidden, context, pre_grad, attend_grad):
    local, width = hidden.shape
    steps = pre_grad.shape[1] // width
    whole = lambda shape: pl.BlockSpec(shape, lambda s: (0, 0))
    out_spec = pl.BlockSpec((width // 2, width), lambda s: (0, s))
    shape = jax.ShapeDtypeStruct((width // 2, (steps + 1) * width), BF16)
    return pl.pallas_call(
        up_kernel,
        grid=(steps + 1,),
        out_shape=(shape, shape),
        in_specs=[
            whole((width, width)),
            whole((local, width)),
            whole((local, width)),
            pl.BlockSpec((local, width), lambda s: (0, jnp.minimum(s, steps - 1))),
            whole((local, width)),
        ],
        out_specs=(out_spec, out_spec),
        scratch_shapes=[pltpu.VMEM((width, local), BF16)],
        compiler_params=params(40),
        cost_estimate=pl.CostEstimate(
            flops=2 * local * width * (steps + 3) * width, bytes_accessed=12 * MIB, transcendentals=0
        ),
        name="up_weight_grad",
    )(order, hidden, context, pre_grad, attend_grad)


def down_kernel(spots, act_ref, grad_ref, keep_ref, send_ref, *, piece):
    step = pl.program_id(0)
    width = act_ref.shape[1]
    half = keep_ref.shape[0]
    value = dot_tn(act_ref[...], grad_ref[...]).astype(BF16)
    for block in range(width // piece):
        spot = spots[step * (width // piece) + block]
        rows = value[block * piece : (block + 1) * piece, :]

        def keep(spot=spot, rows=rows):
            keep_ref[pl.ds(pl.multiple_of(spot, 16), piece), :] = rows

        def send(spot=spot, rows=rows):
            send_ref[pl.ds(pl.multiple_of(spot - half, 16), piece), :] = rows

        pl.when(spot < half)(keep)
        pl.when(spot >= half)(send)


def down_weight_grad(spots, act, grad, piece):
    local, deep = act.shape
    width = grad.shape[1]
    shape = jax.ShapeDtypeStruct((deep // 2, width), BF16)
    out_spec = pl.BlockSpec((deep // 2, width), lambda s: (0, 0))
    return pl.pallas_call(
        functools.partial(down_kernel, piece=piece),
        grid=(deep // width,),
        out_shape=(shape, shape),
        in_specs=[
            smem(),
            pl.BlockSpec((local, width), lambda s: (0, s)),
            pl.BlockSpec((local, width), lambda s: (0, 0)),
        ],
        out_specs=(out_spec, out_spec),
        compiler_params=params(40),
        cost_estimate=pl.CostEstimate(
            flops=2 * local * width * deep, bytes_accessed=8 * MIB, transcendentals=0
        ),
        name="down_weight_grad",
    )(spots, act, grad)


def mixed_back_kernel(
    scalars, ranks_ref, dq_ref, dk_ref, dv_ref, weight_ref, resid_ref, own_ref, other_ref,
    grad_ref, send_ref, taps_ref, cells_ref, sorted_grad, whole, text, patch, masks, edge,
):
    side, fine = scalars[0], scalars[2]
    local, width = own_ref.shape
    seq, part = dq_ref.shape
    groups = width // 128
    pad = GRID_HI + 2
    for start, size in row_chunks(seq, 240):
        total = None
        for block, ref in enumerate((dq_ref, dk_ref, dv_ref)):
            cols = pl.ds(pl.multiple_of(block * width + side * part, 128), part)
            product = dot_nt(ref[start : start + size, :], weight_ref[:, cols])
            total = product if total is None else total + product
        sorted_grad[start : start + size, :] = total
    unsort_rows(ranks_ref, sorted_grad, whole, seq)
    mine = pl.ds(pl.multiple_of(side * local, 8), local)
    theirs = pl.ds(pl.multiple_of((1 - side) * local, 8), local)
    whole[mine, :] = whole[mine, :] + resid_ref[...]
    inner = pl.ds(pl.multiple_of(local - 8 + side * 8, 8), 8)
    outer = pl.ds(pl.multiple_of(local - side * 8, 8), 8)
    edge[0:local, :] = whole[theirs, :]
    edge[local : local + 8, :] = whole[inner, :]
    send_ref[...] = edge[...].astype(BF16)
    grad_ref[0:local, :] = whole[mine, :]
    grad_ref[local : local + 8, :] = whole[outer, :]
    place_slots(own_ref, other_ref, side, text, patch, pad)
    clear_pads(text, patch, pad)
    store_masks(masks, fine, seq - TEXT)
    taps_ref[...] = jnp.zeros(taps_ref.shape, F32)
    cells_ref[...] = jnp.zeros(cells_ref.shape, F32)
    for lane in range(groups):
        cols = slice(lane * 128, lane * 128 + 128)
        for offset in range(-3, 4):
            total = None
            for start, size in row_chunks(TEXT, ROWS):
                value = jnp.sum(
                    whole[start : start + size, cols]
                    * text[lane, pl.ds(8 + start + offset, size), :],
                    axis=0, keepdims=True,
                )
                total = value if total is None else total + value
            for number, (reach, direction) in enumerate(tap_list):
                if reach * direction == offset:
                    taps_ref[number : number + 1, cols] = total
    for grid, chosen in ((GRID_HI, fine != 0), (GRID_LO, fine == 0)):

        def cells(grid=grid):
            for lane in range(groups):
                cols = slice(lane * 128, lane * 128 + 128)
                for number, (down, across) in enumerate(cell_list):
                    moved = patch[lane, pl.ds(pad + down * grid + across, seq - TEXT), :]
                    cells_ref[number : number + 1, cols] = jnp.sum(
                        whole[TEXT:seq, cols] * (moved * masks[number]), axis=0, keepdims=True
                    )

        pl.when(chosen)(cells)


def mixed_back(scalars, ranks, dq, dk, dv, qkv_weight, resid_grad, own, other):
    local, width = own.shape
    seq = ranks.shape[0]
    groups = width // 128
    return pl.pallas_call(
        mixed_back_kernel,
        out_shape=(
            jax.ShapeDtypeStruct((local + 8, width), F32),
            jax.ShapeDtypeStruct((local + 8, width), BF16),
            jax.ShapeDtypeStruct((16, width), F32),
            jax.ShapeDtypeStruct((16, width), F32),
        ),
        in_specs=[smem(), smem()] + [vmem()] * 7,
        out_specs=(vmem(),) * 4,
        scratch_shapes=[
            pltpu.VMEM((seq, width), F32),
            pltpu.VMEM((seq, width), F32),
            pltpu.VMEM((groups, TEXT + 16, 128), F32),
            pltpu.VMEM((groups, seq - TEXT + 2 * (GRID_HI + 2), 128), F32),
            pltpu.VMEM((9, seq - TEXT, 128), F32),
            pltpu.VMEM((local + 8, width), F32),
        ],
        compiler_params=params(40),
        cost_estimate=pl.CostEstimate(
            flops=2 * seq * width * 3 * width // 2, bytes_accessed=12 * MIB, transcendentals=0
        ),
        name="mixed_back",
    )(scalars, ranks, dq, dk, dv, qkv_weight, resid_grad, own, other)


def token_kernel(
    scalars, grad_ref, received_ref, text_kernel, patch_kernel, out_ref, text, patch, masks, lanes
):
    side, fine = scalars[0], scalars[2]
    local, width = out_ref.shape
    groups = width // 128
    pad = GRID_HI + 2
    rows = masks.shape[1]
    head = TEXT - local
    clear_pads(text, patch, pad)
    store_masks(masks, fine, rows)

    def load(low):
        for lane in range(groups):
            cols = slice(lane * 128, lane * 128 + 128)
            total = grad_ref[:, cols] + received_ref[:, cols].astype(F32)
            if low:
                text[lane, 8 : 8 + local + 8, :] = total
                text[lane, 16 + local : 8 + TEXT, :] = jnp.zeros((head - 8, 128), F32)
                patch[lane, pad : pad + rows, :] = jnp.zeros((rows, 128), F32)
            else:
                text[lane, 8 : local, :] = jnp.zeros((local - 8, 128), F32)
                text[lane, local : local + 8, :] = total[local:]
                text[lane, 8 + local : 8 + TEXT, :] = total[:head]
                patch[lane, pad : pad + rows, :] = total[head:local]

    pl.when(side == 0)(lambda: load(True))
    pl.when(side != 0)(lambda: load(False))

    def one_lane(lane, carry):
        mix_lane(text, patch, masks, lanes, lane, text_kernel, patch_kernel, fine, pad, True)
        return carry

    lax.fori_loop(0, groups, one_lane, 0)
    mine = pl.ds(pl.multiple_of(side * local, 8), local)
    for lane in range(groups):
        out_ref[:, lane * 128 : lane * 128 + 128] = lanes[lane, mine, :]


def token_back(scalars, grad, received, text_kernel, patch_kernel, seq):
    local, width = grad.shape[0] - 8, grad.shape[1]
    groups = width // 128
    return pl.pallas_call(
        token_kernel,
        out_shape=jax.ShapeDtypeStruct((local, width), F32),
        in_specs=[smem()] + [vmem()] * 4,
        out_specs=vmem(),
        scratch_shapes=[
            pltpu.VMEM((groups, TEXT + 16, 128), F32),
            pltpu.VMEM((groups, seq - TEXT + 2 * (GRID_HI + 2), 128), F32),
            pltpu.VMEM((9, seq - TEXT, 128), F32),
            pltpu.VMEM((groups, seq, 128), F32),
        ],
        compiler_params=params(32),
        cost_estimate=pl.CostEstimate(
            flops=40 * local * width, bytes_accessed=4 * MIB, transcendentals=0
        ),
        name="token_back",
    )(scalars, grad, received, text_kernel, patch_kernel)


def swap(value, stage):
    axis, bit = stage
    count = lax.axis_size(axis)
    return lax.ppermute(value, axis, [(i, i ^ bit) for i in range(count)])


def stage_flag(stage):
    axis, bit = stage
    return (lax.axis_index(axis) & bit) // bit


def block_bit(block, stage, blk_count):
    axis, bit = stage
    shift = bit * blk_count if axis == "page" else bit
    return (block // shift) & 1


def spot_of(block, stages, blk_count):
    spot = jnp.zeros_like(block)
    for stage in stages:
        spot = spot * 2 + (block_bit(block, stage, blk_count) ^ stage_flag(stage))
    return spot


def order_matrix(width, stages, blk_count):
    count = lax.axis_size("page") * blk_count
    piece = width // count
    place = jnp.arange(width, dtype=jnp.int32)
    spot, inside = place // piece, place % piece
    block = jnp.zeros_like(spot)
    for depth, stage in enumerate(stages):
        axis, bit = stage
        shift = bit * blk_count if axis == "page" else bit
        value = ((spot >> (len(stages) - 1 - depth)) & 1) ^ stage_flag(stage)
        block = block + value * shift
    column = block * piece + inside
    return (column[:, None] == jnp.arange(width, dtype=jnp.int32)[None, :]).astype(BF16)


def halve(keep, send, stages):
    total = keep.astype(F32) + swap(send, stages[0]).astype(F32)
    for stage in stages[1:]:
        half = total.shape[0] // 2
        received = swap(total[half:].astype(BF16), stage)
        total = total[:half] + received.astype(F32)
    return total


def halve_lanes(total, stages):
    for stage in stages:
        half = total.shape[1] // 2
        total = total[:, :half] + swap(total[:, half:], stage)
    return total


def per_device(
    tokens,
    patch_count,
    reading_rank,
    boxes,
    text_kernel,
    patch_kernel,
    qkv_weight,
    rank_table,
    box_tables,
    out_weight,
    norm_gains,
    norm_shifts,
    up_weight,
    up_bias,
    down_weight,
    down_bias,
    cotangent,
):
    side = lax.axis_index("blk")
    blk_count = lax.axis_size("blk")
    page_stages = [("page", 1 << n) for n in range(lax.axis_size("page").bit_length() - 1)]
    across = ("blk", 1)
    first_x = page_stages[:1] + [across] + page_stages[1:]
    then_x = page_stages[:2] + [across] + page_stages[2:]
    last_x = page_stages + [across]
    count = patch_count[0]
    ranks = reading_rank[0]
    own = tokens[0]
    local, width = own.shape
    deep = up_bias.shape[0]
    seq = ranks.shape[0]
    heads = HEADS // blk_count
    scalars = jnp.stack(
        [side, TEXT + count, (count == GRID_HI * GRID_HI).astype(jnp.int32), jnp.int32(0)]
    ).astype(jnp.int32)
    other = swap(own, across)

    xy, xyt = onehots(ranks, boxes[:, 0])
    box_spread = np.arange(2 * SPAN) - (SPAN - 1)
    box_rows = jnp.asarray(bucket_rows(box_spread, box_marks, NB2))
    box_turned = jnp.asarray(bucket_rows(-box_spread, box_marks, NB2))
    rank_rows = jnp.asarray(bucket_rows(np.arange(RANK_LANES) - (RANK_MID - 1), rank_marks, NB1))
    rank_shifted = jnp.asarray(bucket_rows(np.arange(RANK_LANES) - RANK_MID, rank_marks, NB1))
    own_rank = lax.dynamic_slice_in_dim(rank_table, side * heads, heads, 0)
    own_box = lax.dynamic_slice_in_dim(box_tables, side * heads, heads, 1)
    rank_vector = dot_nt(own_rank, rank_shifted.astype(BF16))
    box_vector = lax.dot_general(
        own_box, box_turned.astype(BF16), (((2,), (1,)), ((), ())), preferred_element_type=F32
    )
    box_vector = jnp.pad(jnp.swapaxes(box_vector, 0, 1), ((0, 0), (0, 5), (0, RANK_LANES - 2 * SPAN)))
    vectors = jnp.concatenate([rank_vector[:, None, :], box_vector], axis=1)

    mixed, mixed_low, packed = mix_and_project(
        scalars, ranks, own, other, text_kernel, patch_kernel, qkv_weight
    )
    shares, own_context, their_context = attend(scalars, ranks, packed, xy, vectors, local)
    received = swap(their_context, across)
    context = jnp.where(
        side == 0,
        jnp.concatenate([own_context, received], axis=1),
        jnp.concatenate([received, own_context], axis=1),
    )

    places = side * local + jnp.arange(local, dtype=jnp.int32)
    row_alive = (places < TEXT + count).astype(F32)
    resid_one = mixed + dot_nn(context, out_weight)
    hidden_one, normed_one, inv_one = layer_norm(resid_one, norm_gains[0], norm_shifts[0])
    hidden_low = hidden_one.astype(BF16)
    pre_act = dot_nn(hidden_low, up_weight) + up_bias
    act_low = gelu(pre_act).astype(BF16)
    resid_two = hidden_one + dot_nn(act_low, down_weight) + down_bias
    result, normed_two, inv_two = layer_norm(resid_two, norm_gains[1], norm_shifts[1])
    layer_output = (result * row_alive[:, None]).astype(BF16)
    out_grad = cotangent[0].astype(F32) * row_alive[:, None]
    gain_two = jnp.sum(out_grad * normed_two, axis=0)
    shift_two = jnp.sum(out_grad, axis=0)
    resid_two_grad = norm_back(out_grad, normed_two, inv_two, norm_gains[1])
    down_bias_grad = jnp.sum(resid_two_grad, axis=0)
    branch_grad = resid_two_grad.astype(BF16)
    pre_grad = (dot_nt(branch_grad, down_weight) * gelu_slope(pre_act)).astype(BF16)
    up_bias_grad = jnp.sum(pre_grad.astype(F32), axis=0)
    hidden_grad = resid_two_grad + dot_nt(pre_grad, up_weight)
    gain_one = jnp.sum(hidden_grad * normed_one, axis=0)
    shift_one = jnp.sum(hidden_grad, axis=0)
    resid_one_grad = norm_back(hidden_grad, normed_one, inv_one, norm_gains[0])
    attend_grad = resid_one_grad.astype(BF16)
    context_grad = dot_nt(attend_grad, out_weight).astype(BF16)
    part = width // blk_count
    own_part = lax.dynamic_slice_in_dim(context_grad, side * part, part, 1)
    their_part = lax.dynamic_slice_in_dim(context_grad, (1 - side) * part, part, 1)
    received_part = swap(their_part, across)

    order_up = order_matrix(width, first_x, blk_count)
    order_qkv = order_matrix(width, last_x, blk_count)
    devices = lax.axis_size("page") * blk_count
    piece = deep // devices
    blocks = jnp.arange(devices, dtype=jnp.int32)
    spots = spot_of(blocks, then_x, blk_count) * piece
    act_rows = act_low
    if piece % 16:
        place = jnp.arange(deep, dtype=jnp.int32)
        target = spots[place // piece] + place % piece
        act_rows = jnp.zeros_like(act_low).at[:, target].set(act_low, unique_indices=True)
        piece = width // 8
        spots = jnp.arange(deep // piece, dtype=jnp.int32) * piece
    down_sum = halve(*down_weight_grad(spots, act_rows, branch_grad, piece), then_x)
    up_sum = halve(
        *up_weight_grad(order_up, hidden_low, context, pre_grad, attend_grad), first_x
    )

    dq, dk, dv, sums = attend_back(scalars, ranks, own_part, received_part, shares, packed, xy, xyt)
    qkv_keep, qkv_send = project_weight_grad(order_qkv, mixed_low, dq, dk, dv)
    qkv_part = halve(qkv_keep, qkv_send, page_stages)
    grad, outgoing, taps, cells = mixed_back(
        scalars, ranks, dq, dk, dv, qkv_weight, resid_one_grad, own, other
    )
    incoming = swap(outgoing, across)
    token_grad = token_back(scalars, grad, incoming, text_kernel, patch_kernel, seq)
    half = qkv_part.shape[0] // 2
    qkv_low = qkv_part.astype(BF16)
    received_qkv = swap(qkv_low[half:], across).astype(F32)
    kept_qkv = qkv_part[:half]
    low_side = jnp.where(side == 0, kept_qkv, received_qkv)
    high_side = jnp.where(side == 0, received_qkv, kept_qkv)
    pieces = []
    for block in range(3):
        cols = slice(block * part, (block + 1) * part)
        pieces += [low_side[:, cols], high_side[:, cols]]
    qkv_weight_grad = jnp.concatenate(pieces, axis=1)

    small = jnp.concatenate(
        [
            taps[:9],
            cells[:9],
            jnp.stack([gain_one, gain_two, shift_one, shift_two, down_bias_grad]),
            up_bias_grad.reshape(width, deep // width).T,
        ],
        axis=0,
    )
    small = jnp.pad(small, ((0, -small.shape[0] % 8), (0, 0)))
    small = lax.dot_general(
        small, order_up.astype(F32), (((1,), (1,)), ((), ())),
        precision=lax.Precision.HIGHEST, preferred_element_type=F32,
    )
    small = halve_lanes(small, first_x)
    rank_part = jnp.dot(sums[:, 0], rank_rows, precision=lax.Precision.HIGHEST)
    box_part = lax.dot_general(
        sums[:, 1:3, : 2 * SPAN], box_rows, (((2,), (0,)), ((), ())), precision=lax.Precision.HIGHEST
    )
    tables = jnp.concatenate([rank_part, box_part[:, 0], box_part[:, 1]], axis=1)
    for stage in page_stages:
        tables = tables + swap(tables, stage)
    their_tables = swap(tables, across)
    tables = jnp.where(
        side == 0,
        jnp.concatenate([tables, their_tables], axis=0),
        jnp.concatenate([their_tables, tables], axis=0),
    )
    box_tables_grad = jnp.stack([tables[:, NB1 : NB1 + NB2], tables[:, NB1 + NB2 :]])
    return (
        layer_output[None],
        token_grad[None],
        small[:9],
        small[9:18],
        qkv_weight_grad,
        tables[:, :NB1],
        box_tables_grad,
        up_sum[:, deep:],
        small[18:20],
        small[20:22],
        up_sum[:, :deep],
        small[23 : 23 + deep // width].T.reshape(-1),
        down_sum,
        small[22],
    )


def solution(mesh):
    in_specs = (
        P("page", "blk", None),
        P("page"),
        P("page", None),
        P(None, "page", None),
        P(),
        P(),
        P(),
        P(),
        P(),
        P(),
        P(),
        P(),
        P(),
        P(),
        P(),
        P(),
        P("page", "blk", None),
    )
    out_specs = (
        P("page", "blk", None),
        P("page", "blk", None),
        P(None, ("page", "blk")),
        P(None, ("page", "blk")),
        P(("page", "blk"), None),
        P(),
        P(),
        P(("page", "blk"), None),
        P(None, ("page", "blk")),
        P(None, ("page", "blk")),
        P(("page", "blk"), None),
        P(("page", "blk")),
        P(("page", "blk"), None),
        P(("page", "blk")),
    )
    return jax.shard_map(
        per_device, mesh=mesh, in_specs=in_specs, out_specs=out_specs, check_vma=False
    )
```

time: 1080 us -> 293 us (0.27)
  waiting for transfers between devices: 596 us -> 90 us
  matrix products: 198 us -> 18.5 us
  local copies, waits for them, and re-layouts: 163 us -> 36.5 us
  Pallas kernels: 0 us -> 93.2 us
  other arithmetic: 78 us -> 16.8 us
  starting transfers between devices: 14.9 us -> 32.1 us
  between operations: 16.9 us -> 2.45 us
    reduce_scatter x4 -> x0, waiting for transfers between devices: 506 us -> none  [the longest x1 142 us: per_device(): lax.psum_scatter(up_weight_grad, ('page', 'blk'), scatter_dimension=0, ti...]
    dot_general x24 -> x11, matrix products: 198 us -> 18.5 us  [the longest x3 7.76 us: dot_nn(): lax.dot_general(left, right, (((1,), (0,)), ((), ())), preferred_element_...]
    pallas_call x0 -> x9, Pallas kernels: none -> 93.2 us  [the longest x1 31.2 us: attend(): pl.pallas_call(attend_kernel, grid=(heads,), out_shape=(jax.ShapeDtypeStr...]
    ppermute x4 -> x29, waiting for transfers between devices: 0.27 us -> 90 us  [swap(): return lax.ppermute(value, axis, [(i, i ^ bit) for i in range(count)])]
    unnamed x10 -> x0, waiting for transfers between devices: 78.1 us -> none
    reshape x3, local copies, waits for them, and re-layouts: 68.7 us -> 3.61 us  [the longest x2 2.3 us: per_device(): up_bias_grad.reshape(width, deep // width)]
    sub x12 -> x0, local copies, waits for them, and re-layouts: 32.8 us -> none  [the longest x4 11.4 us: run_forward(): xbox_ids = bucket(box_x[None, :] - query_x[:, None], box_marks, NB2 // 2)]
    add x7 -> x25, other arithmetic: 26.6 us -> 7.99 us  [the longest x3 5.09 us: halve(): total = keep.astype(F32) + swap(send, stages[0]).astype(F32)]
  transfers between devices with their start and end apart: 12 -> 29, of which waited for: 7 -> 18; matrix products, arithmetic and copies ran while one was open for 29% -> 10% of each run, Pallas kernels for 0% -> 20%
where the time goes in v1:
time: 293 us; the launch traced here: 289 us
  Pallas kernels  93.2 us (32%)
  waiting for transfers between devices  90 us (31%)
  local copies, waits for them, and re-layouts  36.5 us (12%)
  starting transfers between devices  32.1 us (11%)
  matrix products  18.5 us (6%)
  other arithmetic  16.8 us (6%)
    ppermute x29, waiting for transfers between devices, swap(): return lax.ppermute(value, axis, [(i, i ^ bit) for i in range(count)])  90 us
    ppermute x29, starting transfers between devices, swap(): return lax.ppermute(value, axis, [(i, i ^ bit) for i in range(count)])  32.1 us
    pallas_call x1, Pallas kernels, attend(): pl.pallas_call(attend_kernel, grid=(heads,), out_shape=(jax.ShapeDtypeStr...  31.2 us
    pallas_call x1, Pallas kernels, attend_back(): pl.pallas_call(attend_back_kernel, grid=(heads,), out_shape=(jax.ShapeDty...  30.3 us
    unnamed x139, local copies, waits for them, and re-layouts  23.5 us
    dot_general x3, matrix products, dot_nn(): lax.dot_general(left, right, (((1,), (0,)), ((), ())), preferred_element_...  7.76 us
    dot_general x4, matrix products, dot_nt(): lax.dot_general(left, right, (((1,), (1,)), ((), ())), preferred_element_...  7.74 us
    pallas_call x1, Pallas kernels, up_weight_grad(): pl.pallas_call(up_kernel, grid=(steps + 1,), out_shape=(shape, shape), in...  6.92 us
  transfers between devices with their start and end apart: 29, of which 18 were waited for; matrix products, arithmetic and copies ran while one was open for 10% of the time, Pallas kernels for 20%

profile of v1, /device:TPU:0, one launch (start us, length us, event | category | flops | bytes accessed | tf_op | source)
XLA Modules:
  0.0 289.5 jit_solution(2458134564535214998)
XLA Ops:
  0.7 3.0 %collective-permute-start = (bf16[360,768]{1,0:T(8,128)(2,1)}, bf16[360,768]{1,0:T(8,128)(2,1)S(1)}, u32[]{:S(2)}, u32[]{:S(2)}) collective-permute-start(bf16[360,768]{1,0:T(8,128)(2,1)} %bitcast.56), channel_id=1, source_target_pairs={{0,1},{1,0},{2,3},{3,2},{4,5},{5,4},{6,7},{7,6},{8,9},{9,8},{10,11... | collective-permute-start | bytes 1658888 | tf_op jit(solution)/shard_map/ppermute | solution.py:764
  16.4 4.6 %mix_and_project.1 = (f32[360,768]{1,0:T(8,128)S(1)}, bf16[720,768]{1,0:T(8,128)(2,1)S(1)}, bf16[720,1152]{1,0:T(8,128)(2,1)S(1)}) custom-call(s32[4]{0:T(128)S(1)} %pad_add_fusion.scalars.side_ref, s32[720]{0:T(1024)S(1)} %reduce.ranks_ref, bf16[360,768]{1,0:T(8,128)(2,1)S(1)} %bitcast.57, bf16[360,768]{1,0:T(8,128)(2,1)S(1)} %collective-permute-done.other_ref, ...), custom_call_target="tpu_custom_call" | custom-call | flops 1274019840 | bytes 12582912 | tf_op jit(solution)/shard_map/mix_and_project/pallas_call | solution.py:271
  23.1 31.2 %attend.1 = (bf16[6,720,720]{2,1,0:T(8,128)(2,1)S(1)}, bf16[360,384]{1,0:T(8,128)(2,1)S(1)}, bf16[360,384]{1,0:T(8,128)(2,1)}) custom-call(s32[4]{0:T(128)S(1)} %pad_add_fusion.scalars.side_ref, s32[720]{0:T(1024)S(1)} %reduce.ranks_ref, bf16[720,1152]{1,0:T(8,128)(2,1)S(1)} %get-tuple-element.37.queries.keys.values, ...), custom_call_target="tpu_custom_call" | custom-call | flops 6370099200 | bytes 6220800 | tf_op jit(solution)/shard_map/attend/pallas_call | solution.py:356
  54.3 2.7 copy-done.44
  57.1 1.8 collective-permute-start.1
  60.2 5.0 %collective-permute-done.1 = bf16[360,384]{1,0:T(8,128)(2,1)} collective-permute-done((bf16[360,384]{1,0:T(8,128)(2,1)}, bf16[360,384]{1,0:T(8,128)(2,1)}, u32[]{:S(2)}, u32[]{:S(2)}) %collective-permute-start.1) | collective-permute-done | bytes 276512 | tf_op jit(solution)/shard_map/ppermute | solution.py:764
  68.9 5.0 %multiply_convert_fusion = (bf16[360,3072]{1,0:T(8,128)(2,1)S(1)}, f32[360,3072]{1,0:T(8,128)S(1)}) fusion(f32[3072]{0:T(1024)S(1)} %copy-done.60, bf16[360,768]{1,0:T(8,128)(2,1)S(1)} %fusion.21.hidden_ref, bf16[768,3072]{1,0:T(8,128)(2,1)} %param.33), kind=kOutput, calls=%fused_computation.10 | convolution fusion | flops 1705328640 | bytes 11919360 | tf_op jit(solution)/shard_map/dot_general | solution.py:71
  74.0 2.1 fusion.68
  79.3 3.5 %convert_reduce_fusion = (f32[3072]{0:T(1024)S(1)}, bf16[360,3072]{1,0:T(8,128)(2,1)S(1)}) fusion(f32[360,3072]{1,0:T(8,128)S(1)} %get-tuple-element.118, bf16[360,768]{1,0:T(8,128)(2,1)S(1)} %convert_element_type.135.grad_ref, bf16[3072,768]{1,0:T(8,128)(2,1)S(1)} %bitcast.66), kind=kOutput, calls=%fused_computation.9 | convolution fusion | flops 1711961088 | bytes 11919360 | tf_op jit(solution)/shard_map/dot_general | solution.py:75
  82.9 2.3 multiply_reduce_fusion
  87.3 1.4 collective-permute-start.2
  93.4 1.6 copy-done.39
  95.0 6.9 %up_weight_grad.1 = (bf16[384,3840]{1,0:T(8,128)(2,1)S(1)}, bf16[384,3840]{1,0:T(8,128)(2,1)}) custom-call(bf16[768,768]{1,0:T(8,128)(2,1)S(1)} %copy-done.10, bf16[360,768]{1,0:T(8,128)(2,1)S(1)} %copy-done.24, bf16[360,768]{1,0:T(8,128)(2,1)S(1)} %copy-done.8, bf16[360,3072]{1,0:T(8,128)(2,1)S(1)} %copy-done.39, bf16[360,768]{1,0:T(8,128)(2,1)S(1)} %copy-done.26), custom_call_target="tpu_custom_call" | custom-call | flops 2972712960 | bytes 12582912 | tf_op jit(solution)/shard_map/up_weight_grad/pallas_call | solution.py:547
  102.0 1.6 copy-done.4
  103.6 2.9 copy-done.45
  106.5 30.3 %attend_back.1 = (bf16[720,384]{1,0:T(8,128)(2,1)S(1)}, bf16[720,384]{1,0:T(8,128)(2,1)S(1)}, bf16[720,384]{1,0:T(8,128)(2,1)S(1)}, f32[6,8,1536]{2,1,0:T(8,128)S(1)}) custom-call(s32[720]{0:T(1024)S(1)} %reduce.ranks_ref, bf16[360,384]{1,0:T(8,128)(2,1)S(1)} %copy-done.27, bf16[360,384]{1,0:T(8,128)(2,1)} %collective-permute-done.2.other_ref, ...), custom_call_target="tpu_custom_call" | custom-call | flops 9953280000 | bytes 6220800 | tf_op jit(solution)/shard_map/attend_back/pallas_call | solution.py:459
  138.2 5.5 %mixed_back.1 = (f32[368,768]{1,0:T(8,128)S(1)}, bf16[368,768]{1,0:T(8,128)(2,1)}, f32[16,768]{1,0:T(8,128)S(1)}, f32[16,768]{1,0:T(8,128)S(1)}) custom-call(s32[4]{0:T(128)S(1)} %pad_add_fusion.scalars.side_ref, s32[720]{0:T(1024)S(1)} %reduce.ranks_ref, bf16[720,384]{1,0:T(8,128)(2,1)S(1)} %get-tuple-element.43.dq_ref, ...), custom_call_target="tpu_custom_call" | custom-call | flops 1274019840 | bytes 12582912 | tf_op jit(solution)/shard_map/mixed_back/pallas_call | solution.py:674
  145.1 1.6 collective-permute-start.15
  148.7 1.7 collective-permute-start.16
  151.5 1.6 copy-done.43
  153.1 6.2 %down_weight_grad.1 = (bf16[1536,768]{1,0:T(8,128)(2,1)S(1)}, bf16[1536,768]{1,0:T(8,128)(2,1)}) custom-call(s32[32]{0:T(128)S(1)} %fusion.60.spots, bf16[360,3072]{1,0:T(8,128)(2,1)S(1)} %copy-done.43, bf16[360,768]{1,0:T(8,128)(2,1)S(1)} %copy-done.22), custom_call_target="tpu_custom_call" | custom-call | flops 1698693120 | bytes 8388608 | tf_op jit(solution)/shard_map/down_weight_grad/pallas_call | solution.py:592
  159.8 2.5 collective-permute-start.17
  162.4 1.5 collective-permute-start.5
  163.9 3.4 %project_weight_grad.1 = (bf16[384,1152]{1,0:T(8,128)(2,1)S(1)}, bf16[384,1152]{1,0:T(8,128)(2,1)S(1)}) custom-call(bf16[768,768]{1,0:T(8,128)(2,1)S(1)} %copy-done.9, bf16[720,768]{1,0:T(8,128)(2,1)S(1)} %copy-done.35, bf16[720,384]{1,0:T(8,128)(2,1)S(1)} %copy-done.16, bf16[720,384]{1,0:T(8,128)(2,1)S(1)} %copy-done.18, bf16[720,384]{1,0:T(8,128)(2,1)S(1)} %copy-done.20), custom_call_target="tpu_custom_call" | custom-call | flops 2123366400 | bytes 8388608 | tf_op jit(solution)/shard_map/project_weight_grad/pallas_call | solution.py:507
  167.4 8.0 %collective-permute-done.5 = f32[32,192]{1,0:T(8,128)S(1)} collective-permute-done((f32[32,192]{1,0:T(8,128)S(1)}, f32[32,192]{1,0:T(8,128)S(1)}, u32[]{:S(2)}, u32[]{:S(2)}) %collective-permute-start.5) | collective-permute-done | bytes 24608 | tf_op jit(solution)/shard_map/ppermute | solution.py:764
  176.0 3.0 %collective-permute-done.18 = f32[6,160]{1,0:T(8,128)S(1)} collective-permute-done((f32[6,160]{1,0:T(8,128)S(1)}, f32[6,160]{1,0:T(8,128)S(1)}, u32[]{:S(2)}, u32[]{:S(2)}) %collective-permute-start.18) | collective-permute-done | bytes 3872 | tf_op jit(solution)/shard_map/ppermute | solution.py:764
  179.1 1.5 collective-permute-start.6
  180.6 2.2 collective-permute-done.6
  183.6 3.0 %collective-permute-done.7 = f32[32,48]{1,0:T(8,128)S(1)} collective-permute-done((f32[32,48]{1,0:T(8,128)S(1)}, f32[32,48]{1,0:T(8,128)S(1)}, u32[]{:S(2)}, u32[]{:S(2)}) %collective-permute-start.7) | collective-permute-done | bytes 6176 | tf_op jit(solution)/shard_map/ppermute | solution.py:764
  186.7 2.5 collective-permute-start.8
  191.7 1.5 collective-permute-start.10
  194.4 5.7 %collective-permute-done.10 = bf16[192,1152]{1,0:T(8,128)(2,1)S(1)} collective-permute-done((bf16[192,1152]{1,0:T(8,128)(2,1)S(1)}, bf16[192,1152]{1,0:T(8,128)(2,1)S(1)}, u32[]{:S(2)}, u32[]{:S(2)}) %collective-permute-start.10) | collective-permute-done | bytes 442400 | tf_op jit(solution)/shard_map/ppermute | solution.py:764
  201.0 6.4 %collective-permute-done.11 = bf16[96,1152]{1,0:T(8,128)(2,1)S(1)} collective-permute-done((bf16[96,1152]{1,0:T(8,128)(2,1)S(1)}, bf16[96,1152]{1,0:T(8,128)(2,1)S(1)}, u32[]{:S(2)}, u32[]{:S(2)}) %collective-permute-start.11) | collective-permute-done | bytes 221216 | tf_op jit(solution)/shard_map/ppermute | solution.py:764
  208.8 1.5 collective-permute-start.12
  213.7 4.1 %token_back.1 = f32[360,768]{1,0:T(8,128)} custom-call(s32[4]{0:T(128)S(1)} %pad_add_fusion.scalars.side_ref, f32[368,768]{1,0:T(8,128)S(1)} %copy-done.12, bf16[368,768]{1,0:T(8,128)(2,1)} %collective-permute-done.3.received_ref, f32[9,768]{1,0:T(8,128)S(1)} %copy-done.28, f32[9,768]{1,0:T(8,128)S(1)} %copy-done.30), custom_call_target="tpu_custom_call" | custom-call | flops 11059200 | bytes 4194304 | tf_op jit(solution)/shard_map/token_back/pallas_call | solution.py:742
  219.3 2.3 convert_add_fusion.1
  221.7 1.6 collective-permute-start.25
  223.3 2.6 convert_add_fusion
  226.1 1.6 collective-permute-start.20
  227.7 14.4 %collective-permute-done.25 = bf16[768,768]{1,0:T(8,128)(2,1)S(1)} collective-permute-done((bf16[768,768]{1,0:T(8,128)(2,1)S(1)}, bf16[768,768]{1,0:T(8,128)(2,1)S(1)}, u32[]{:S(2)}, u32[]{:S(2)}) %collective-permute-start.25) | collective-permute-done | bytes 1179680 | tf_op jit(solution)/shard_map/ppermute | solution.py:764
  242.4 1.5 collective-permute-start.26
  244.0 15.4 %collective-permute-done.20 = bf16[192,3840]{1,0:T(8,128)(2,1)S(1)} collective-permute-done((bf16[192,3840]{1,0:T(8,128)(2,1)S(1)}, bf16[192,3840]{1,0:T(8,128)(2,1)S(1)}, u32[]{:S(2)}, u32[]{:S(2)}) %collective-permute-start.20) | collective-permute-done | bytes 1474592 | tf_op jit(solution)/shard_map/ppermute | solution.py:764
  260.4 5.3 %collective-permute-done.26 = bf16[384,768]{1,0:T(8,128)(2,1)S(1)} collective-permute-done((bf16[384,768]{1,0:T(8,128)(2,1)S(1)}, bf16[384,768]{1,0:T(8,128)(2,1)S(1)}, u32[]{:S(2)}, u32[]{:S(2)}) %collective-permute-start.26) | collective-permute-done | bytes 589856 | tf_op jit(solution)/shard_map/ppermute | solution.py:764
  266.7 4.6 %collective-permute-done.21 = bf16[96,3840]{1,0:T(8,128)(2,1)S(1)} collective-permute-done((bf16[96,3840]{1,0:T(8,128)(2,1)S(1)}, bf16[96,3840]{1,0:T(8,128)(2,1)S(1)}, u32[]{:S(2)}, u32[]{:S(2)}) %collective-permute-start.21) | collective-permute-done | bytes 737312 | tf_op jit(solution)/shard_map/ppermute | solution.py:764
  272.4 2.9 collective-permute-done.27
  275.5 3.8 %collective-permute-done.22 = bf16[48,3840]{1,0:T(8,128)(2,1)S(1)} collective-permute-done((bf16[48,3840]{1,0:T(8,128)(2,1)S(1)}, bf16[48,3840]{1,0:T(8,128)(2,1)S(1)}, u32[]{:S(2)}, u32[]{:S(2)}) %collective-permute-start.22) | collective-permute-done | bytes 368672 | tf_op jit(solution)/shard_map/ppermute | solution.py:764
  280.1 2.6 collective-permute-done.28
  283.4 4.5 %collective-permute-done.23 = bf16[24,3840]{1,0:T(8,128)(2,1)S(1)} collective-permute-done((bf16[24,3840]{1,0:T(8,128)(2,1)S(1)}, bf16[24,3840]{1,0:T(8,128)(2,1)S(1)}, u32[]{:S(2)}, u32[]{:S(2)}) %collective-permute-start.23) | collective-permute-done | bytes 184352 | tf_op jit(solution)/shard_map/ppermute | solution.py:764
  (268 shorter events, 54.5 us)
Async XLA Ops:
  0.6 65.8 %copy-start = (bf16[768,768]{1,0:T(8,128)(2,1)S(1)}, bf16[768,768]{1,0:T(8,128)(2,1)}, u32[]{:S(2)}) copy-start(bf16[768,768]{1,0:T(8,128)(2,1)} %param.30) | copy-start | bytes 3538948
  0.7 15.8 %collective-permute-start = (bf16[360,768]{1,0:T(8,128)(2,1)}, bf16[360,768]{1,0:T(8,128)(2,1)S(1)}, u32[]{:S(2)}, u32[]{:S(2)}) collective-permute-start(bf16[360,768]{1,0:T(8,128)(2,1)} %bitcast.56), channel_id=1, source_target_pairs={{0,1},{1,0},{2,3},{3,2},{4,5},{5,4},{6,7},{7,6},{8,9},{9,8},{10,11... | collective-permute-start | bytes 1658888 | tf_op jit(solution)/shard_map/ppermute | solution.py:764
  3.7 55.2 %copy-start.57 = (s32[768]{0:T(1024)}, s32[768]{0:T(1024)S(1)}, u32[]{:S(2)}) copy-start(s32[768]{0:T(1024)S(1)} %fusion.34) | copy-start | bytes 9220
  5.1 11.4 %copy-start.29 = (f32[9,768]{1,0:T(8,128)S(1)}, f32[9,768]{1,0:T(8,128)}, u32[]{:S(2)}) copy-start(f32[9,768]{1,0:T(8,128)} %patch_kernel.3) | copy-start | bytes 82948
  6.0 10.4 %copy-start.6 = (bf16[1,360,768]{2,1,0:T(8,128)(2,1)S(1)}, bf16[1,360,768]{2,1,0:T(8,128)(2,1)}, u32[]{:S(2)}) copy-start(bf16[1,360,768]{2,1,0:T(8,128)(2,1)} %param.21) | copy-start | bytes 1658884
  8.7 59.7 %copy-start.51 = (f32[768]{0:T(1024)}, f32[768]{0:T(1024)S(1)}, u32[]{:S(2)}) copy-start(f32[768]{0:T(1024)S(1)} %get-tuple-element.124) | copy-start | bytes 9220
  8.7 59.7 %copy-start.55 = (f32[768]{0:T(1024)}, f32[768]{0:T(1024)S(1)}, u32[]{:S(2)}) copy-start(f32[768]{0:T(1024)S(1)} %get-tuple-element.97) | copy-start | bytes 9220
  13.7 9.4 %copy-start.40 = (bf16[720,512]{1,0:T(8,128)(2,1)}, bf16[720,512]{1,0:T(8,128)(2,1)S(1)}, u32[]{:S(2)}) copy-start(bf16[720,512]{1,0:T(8,128)(2,1)S(1)} %get-tuple-element.38.xy_ref) | copy-start | bytes 2211844
  23.1 31.2 %copy-start.32 = (bf16[720,1152]{1,0:T(8,128)(2,1)}, bf16[720,1152]{1,0:T(8,128)(2,1)S(1)}, u32[]{:S(2)}) copy-start(bf16[720,1152]{1,0:T(8,128)(2,1)S(1)} %get-tuple-element.37.queries.keys.values) | copy-start | bytes 4976644
  57.1 8.2 %collective-permute-start.1 = (bf16[360,384]{1,0:T(8,128)(2,1)}, bf16[360,384]{1,0:T(8,128)(2,1)}, u32[]{:S(2)}, u32[]{:S(2)}) collective-permute-start(bf16[360,384]{1,0:T(8,128)(2,1)} %get-tuple-element.40), channel_id=1, source_target_pairs={{0,1},{1,0},{2,3},{3,2},{4,5},{5,4},{6,7},{7,6},{8,9},{9,8},{10,11... | collective-permute-start | bytes 829448 | tf_op jit(solution)/shard_map/ppermute | solution.py:764
  87.3 16.3 %collective-permute-start.2 = (bf16[360,384]{1,0:T(8,128)(2,1)}, bf16[360,384]{1,0:T(8,128)(2,1)}, u32[]{:S(2)}, u32[]{:S(2)}) collective-permute-start(bf16[360,384]{1,0:T(8,128)(2,1)} %get-tuple-element.105), channel_id=1, source_target_pairs={{0,1},{1,0},{2,3},{3,2},{4,5},{5,4},{6,7},{7,6},{8,9},{9,8},{10,11... | collective-permute-start | bytes 829448 | tf_op jit(solution)/shard_map/ppermute | solution.py:764
  95.0 8.5 %copy-start.41 = (bf16[720,512]{1,0:T(8,128)(2,1)S(1)}, bf16[720,512]{1,0:T(8,128)(2,1)}, u32[]{:S(2)}) copy-start(bf16[720,512]{1,0:T(8,128)(2,1)} %copy-done.40) | copy-start | bytes 2211844
  103.5 119.8 %collective-permute-start.19 = (bf16[384,3840]{1,0:T(8,128)(2,1)}, bf16[384,3840]{1,0:T(8,128)(2,1)}, u32[]{:S(2)}, u32[]{:S(2)}) collective-permute-start(bf16[384,3840]{1,0:T(8,128)(2,1)} %get-tuple-element.55), channel_id=1, source_target_pairs={{0,2},{2,0},{4,6},{6,4},{8,10},{10,8},{12,14},{14,12},{16,18},{18,... | collective-permute-start | bytes 8847368 | tf_op jit(solution)/shard_map/ppermute | solution.py:764
  106.5 30.4 %copy-start.50 = (f32[512,64,1]{0,1,2:T(8,128)S(1)}, f32[512,64,1]{0,1,2:T(8,128)}, u32[]{:S(2)}) copy-start(f32[512,64,1]{0,1,2:T(8,128)} %constant.232) | copy-start | bytes 393220
  106.5 30.6 %copy-start.49 = (f32[1536,32]{1,0:T(8,128)S(1)}, f32[1536,32]{1,0:T(8,128)}, u32[]{:S(2)}) copy-start(f32[1536,32]{1,0:T(8,128)} %constant.218.clone) | copy-start | bytes 589828
  106.5 31.7 %copy-start.3 = (bf16[768,2304]{1,0:T(8,128)(2,1)S(1)}, bf16[768,2304]{1,0:T(8,128)(2,1)}, u32[]{:S(2)}) copy-start(bf16[768,2304]{1,0:T(8,128)(2,1)} %weight_ref.3) | copy-start | bytes 10616836
  137.7 7.3 %collective-permute-start.14 = (f32[6,160]{1,0:T(8,128)S(1)}, f32[6,160]{1,0:T(8,128)S(1)}, u32[]{:S(2)}, u32[]{:S(2)}) collective-permute-start(f32[6,160]{1,0:T(8,128)S(1)} %pad_maximum_fusion.1), channel_id=1, source_target_pairs={{0,2},{2,0},{4,6},{6,4},{8,10},{10,8},{12,14},{14,12},{16,18},{18,... | collective-permute-start | bytes 11528 | tf_op jit(solution)/shard_map/ppermute | solution.py:764
  145.1 3.7 %collective-permute-start.15 = (f32[6,160]{1,0:T(8,128)S(1)}, f32[6,160]{1,0:T(8,128)S(1)}, u32[]{:S(2)}, u32[]{:S(2)}) collective-permute-start(f32[6,160]{1,0:T(8,128)S(1)} %fusion.86), channel_id=1, source_target_pairs={{0,4},{2,6},{4,0},{6,2},{8,12},{10,14},{12,8},{14,10},{16,20},{18,... | collective-permute-start | bytes 11528 | tf_op jit(solution)/shard_map/ppermute | solution.py:764
  147.9 14.4 %collective-permute-start.4 = (f32[32,384]{1,0:T(8,128)S(1)}, f32[32,384]{1,0:T(8,128)S(1)}, u32[]{:S(2)}, u32[]{:S(2)}) collective-permute-start(f32[32,384]{1,0:T(8,128)S(1)} %slice.258), channel_id=1, source_target_pairs={{0,2},{2,0},{4,6},{6,4},{8,10},{10,8},{12,14},{14,12},{16,18},{18,... | collective-permute-start | bytes 147464 | tf_op jit(solution)/shard_map/ppermute | solution.py:764
  148.7 15.2 %copy-start.9 = (bf16[768,768]{1,0:T(8,128)(2,1)S(1)}, bf16[768,768]{1,0:T(8,128)(2,1)}, u32[]{:S(2)}) copy-start(bf16[768,768]{1,0:T(8,128)(2,1)} %fusion.8.order_ref) | copy-start | bytes 3538948
  148.7 15.2 %copy-start.16 = (bf16[720,384]{1,0:T(8,128)(2,1)S(1)}, bf16[720,384]{1,0:T(8,128)(2,1)}, u32[]{:S(2)}) copy-start(bf16[720,384]{1,0:T(8,128)(2,1)} %copy-done.15) | copy-start | bytes 1658884
  148.7 15.2 %copy-start.18 = (bf16[720,384]{1,0:T(8,128)(2,1)S(1)}, bf16[720,384]{1,0:T(8,128)(2,1)}, u32[]{:S(2)}) copy-start(bf16[720,384]{1,0:T(8,128)(2,1)} %copy-done.17) | copy-start | bytes 1658884
  148.7 15.2 %copy-start.20 = (bf16[720,384]{1,0:T(8,128)(2,1)S(1)}, bf16[720,384]{1,0:T(8,128)(2,1)}, u32[]{:S(2)}) copy-start(bf16[720,384]{1,0:T(8,128)(2,1)} %copy-done.19) | copy-start | bytes 1658884
  148.7 11.1 %collective-permute-start.16 = (f32[6,160]{1,0:T(8,128)S(1)}, f32[6,160]{1,0:T(8,128)S(1)}, u32[]{:S(2)}, u32[]{:S(2)}) collective-permute-start(f32[6,160]{1,0:T(8,128)S(1)} %add.330), channel_id=1, source_target_pairs={{0,8},{2,10},{4,12},{6,14},{8,0},{10,2},{12,4},{14,6},{16,24},{18,... | collective-permute-start | bytes 11528 | tf_op jit(solution)/shard_map/ppermute | solution.py:764
  153.1 10.8 %copy-start.35 = (bf16[720,768]{1,0:T(8,128)(2,1)S(1)}, bf16[720,768]{1,0:T(8,128)(2,1)}, u32[]{:S(2)}) copy-start(bf16[720,768]{1,0:T(8,128)(2,1)} %copy-done.34) | copy-start | bytes 3317764
  159.3 60.0 %collective-permute-start.24 = (bf16[1536,768]{1,0:T(8,128)(2,1)}, bf16[1536,768]{1,0:T(8,128)(2,1)}, u32[]{:S(2)}, u32[]{:S(2)}) collective-permute-start(bf16[1536,768]{1,0:T(8,128)(2,1)} %get-tuple-element.57), channel_id=1, source_target_pairs={{0,2},{2,0},{4,6},{6,4},{8,10},{10,8},{12,14},{14,12},{16,18},{18,... | collective-permute-start | bytes 7077896 | tf_op jit(solution)/shard_map/ppermute | solution.py:764
  159.3 53.6 %collective-permute-start.3 = (bf16[368,768]{1,0:T(8,128)(2,1)}, bf16[368,768]{1,0:T(8,128)(2,1)}, u32[]{:S(2)}, u32[]{:S(2)}) collective-permute-start(bf16[368,768]{1,0:T(8,128)(2,1)} %get-tuple-element.47), channel_id=1, source_target_pairs={{0,1},{1,0},{2,3},{3,2},{4,5},{5,4},{6,7},{7,6},{8,9},{9,8},{10,11... | collective-permute-start | bytes 1695752 | tf_op jit(solution)/shard_map/ppermute | solution.py:764
  159.8 7.5 %collective-permute-start.17 = (f32[6,160]{1,0:T(8,128)S(1)}, f32[6,160]{1,0:T(8,128)S(1)}, u32[]{:S(2)}, u32[]{:S(2)}) collective-permute-start(f32[6,160]{1,0:T(8,128)S(1)} %add.331), channel_id=1, source_target_pairs={{0,16},{2,18},{4,20},{6,22},{8,24},{10,26},{12,28},{14,30},{16,0},... | collective-permute-start | bytes 11528 | tf_op jit(solution)/shard_map/ppermute | solution.py:764
  162.4 13.0 %collective-permute-start.5 = (f32[32,192]{1,0:T(8,128)S(1)}, f32[32,192]{1,0:T(8,128)S(1)}, u32[]{:S(2)}, u32[]{:S(2)}) collective-permute-start(f32[32,192]{1,0:T(8,128)S(1)} %slice.260), channel_id=1, source_target_pairs={{0,1},{1,0},{2,3},{3,2},{4,5},{5,4},{6,7},{7,6},{8,9},{9,8},{10,11... | collective-permute-start | bytes 73736 | tf_op jit(solution)/shard_map/ppermute | solution.py:764
  167.3 24.0 %collective-permute-start.9 = (bf16[384,1152]{1,0:T(8,128)(2,1)S(1)}, bf16[384,1152]{1,0:T(8,128)(2,1)S(1)}, u32[]{:S(2)}, u32[]{:S(2)}) collective-permute-start(bf16[384,1152]{1,0:T(8,128)(2,1)S(1)} %get-tuple-element.52), channel_id=1, source_target_pairs={{0,2},{2,0},{4,6},{6,4},{8,10},{10,8},{12,14},{14,12},{16,18},{18,... | collective-permute-start | bytes 2654216 | tf_op jit(solution)/shard_map/ppermute | solution.py:764
  175.4 3.7 %collective-permute-start.18 = (f32[6,160]{1,0:T(8,128)S(1)}, f32[6,160]{1,0:T(8,128)S(1)}, u32[]{:S(2)}, u32[]{:S(2)}) collective-permute-start(f32[6,160]{1,0:T(8,128)S(1)} %add.332), channel_id=1, source_target_pairs={{0,1},{1,0},{2,3},{3,2},{4,5},{5,4},{6,7},{7,6},{8,9},{9,8},{10,11... | collective-permute-start | bytes 11528 | tf_op jit(solution)/shard_map/ppermute | solution.py:764
  179.1 3.7 %collective-permute-start.6 = (f32[32,96]{1,0:T(8,128)S(1)}, f32[32,96]{1,0:T(8,128)S(1)}, u32[]{:S(2)}, u32[]{:S(2)}) collective-permute-start(f32[32,96]{1,0:T(8,128)S(1)} %slice.262), channel_id=1, source_target_pairs={{0,4},{2,6},{4,0},{6,2},{8,12},{10,14},{12,8},{14,10},{16,20},{18,... | collective-permute-start | bytes 36872 | tf_op jit(solution)/shard_map/ppermute | solution.py:764
  182.9 3.8 %collective-permute-start.7 = (f32[32,48]{1,0:T(8,128)S(1)}, f32[32,48]{1,0:T(8,128)S(1)}, u32[]{:S(2)}, u32[]{:S(2)}) collective-permute-start(f32[32,48]{1,0:T(8,128)S(1)} %slice.264), channel_id=1, source_target_pairs={{0,8},{2,10},{4,12},{6,14},{8,0},{10,2},{12,4},{14,6},{16,24},{18,... | collective-permute-start | bytes 18440 | tf_op jit(solution)/shard_map/ppermute | solution.py:764
  186.7 4.7 %collective-permute-start.8 = (f32[32,24]{1,0:T(8,128)S(1)}, f32[32,24]{1,0:T(8,128)S(1)}, u32[]{:S(2)}, u32[]{:S(2)}) collective-permute-start(f32[32,24]{1,0:T(8,128)S(1)} %slice.266), channel_id=1, source_target_pairs={{0,16},{2,18},{4,20},{6,22},{8,24},{10,26},{12,28},{14,30},{16,0},... | collective-permute-start | bytes 9224 | tf_op jit(solution)/shard_map/ppermute | solution.py:764
  191.7 8.4 %collective-permute-start.10 = (bf16[192,1152]{1,0:T(8,128)(2,1)S(1)}, bf16[192,1152]{1,0:T(8,128)(2,1)S(1)}, u32[]{:S(2)}, u32[]{:S(2)}) collective-permute-start(bf16[192,1152]{1,0:T(8,128)(2,1)S(1)} %slice.360), channel_id=1, source_target_pairs={{0,4},{2,6},{4,0},{6,2},{8,12},{10,14},{12,8},{14,10},{16,20},{18,... | collective-permute-start | bytes 1327112 | tf_op jit(solution)/shard_map/ppermute | solution.py:764
  200.1 12.8 %copy-start.12 = (f32[368,768]{1,0:T(8,128)S(1)}, f32[368,768]{1,0:T(8,128)}, u32[]{:S(2)}) copy-start(f32[368,768]{1,0:T(8,128)} %copy-done.11) | copy-start | bytes 3391492
  200.2 7.2 %collective-permute-start.11 = (bf16[96,1152]{1,0:T(8,128)(2,1)S(1)}, bf16[96,1152]{1,0:T(8,128)(2,1)S(1)}, u32[]{:S(2)}, u32[]{:S(2)}) collective-permute-start(bf16[96,1152]{1,0:T(8,128)(2,1)S(1)} %slice.363), channel_id=1, source_target_pairs={{0,8},{2,10},{4,12},{6,14},{8,0},{10,2},{12,4},{14,6},{16,24},{18,... | collective-permute-start | bytes 663560 | tf_op jit(solution)/shard_map/ppermute | solution.py:764
  208.8 8.9 %collective-permute-start.12 = (bf16[48,1152]{1,0:T(8,128)(2,1)}, bf16[48,1152]{1,0:T(8,128)(2,1)}, u32[]{:S(2)}, u32[]{:S(2)}) collective-permute-start(bf16[48,1152]{1,0:T(8,128)(2,1)} %slice.366), channel_id=1, source_target_pairs={{0,16},{2,18},{4,20},{6,22},{8,24},{10,26},{12,28},{14,30},{16,0},... | collective-permute-start | bytes 331784 | tf_op jit(solution)/shard_map/ppermute | solution.py:764
  218.7 8.9 %collective-permute-start.13 = (bf16[24,1152]{1,0:T(8,128)(2,1)S(1)}, bf16[24,1152]{1,0:T(8,128)(2,1)S(1)}, u32[]{:S(2)}, u32[]{:S(2)}) collective-permute-start(bf16[24,1152]{1,0:T(8,128)(2,1)S(1)} %slice.367), channel_id=1, source_target_pairs={{0,1},{1,0},{2,3},{3,2},{4,5},{5,4},{6,7},{7,6},{8,9},{9,8},{10,11... | collective-permute-start | bytes 165896 | tf_op jit(solution)/shard_map/ppermute | solution.py:764
  221.7 20.4 %collective-permute-start.25 = (bf16[768,768]{1,0:T(8,128)(2,1)S(1)}, bf16[768,768]{1,0:T(8,128)(2,1)S(1)}, u32[]{:S(2)}, u32[]{:S(2)}) collective-permute-start(bf16[768,768]{1,0:T(8,128)(2,1)S(1)} %slice.357), channel_id=1, source_target_pairs={{0,4},{2,6},{4,0},{6,2},{8,12},{10,14},{12,8},{14,10},{16,20},{18,... | collective-permute-start | bytes 3538952 | tf_op jit(solution)/shard_map/ppermute | solution.py:764
  226.1 33.3 %collective-permute-start.20 = (bf16[192,3840]{1,0:T(8,128)(2,1)S(1)}, bf16[192,3840]{1,0:T(8,128)(2,1)S(1)}, u32[]{:S(2)}, u32[]{:S(2)}) collective-permute-start(bf16[192,3840]{1,0:T(8,128)(2,1)S(1)} %slice.356), channel_id=1, source_target_pairs={{0,1},{1,0},{2,3},{3,2},{4,5},{5,4},{6,7},{7,6},{8,9},{9,8},{10,11... | collective-permute-start | bytes 4423688 | tf_op jit(solution)/shard_map/ppermute | solution.py:764
  242.4 23.3 %collective-permute-start.26 = (bf16[384,768]{1,0:T(8,128)(2,1)S(1)}, bf16[384,768]{1,0:T(8,128)(2,1)S(1)}, u32[]{:S(2)}, u32[]{:S(2)}) collective-permute-start(bf16[384,768]{1,0:T(8,128)(2,1)S(1)} %slice.359), channel_id=1, source_target_pairs={{0,1},{1,0},{2,3},{3,2},{4,5},{5,4},{6,7},{7,6},{8,9},{9,8},{10,11... | collective-permute-start | bytes 1769480 | tf_op jit(solution)/shard_map/ppermute | solution.py:764
  259.8 11.5 %collective-permute-start.21 = (bf16[96,3840]{1,0:T(8,128)(2,1)S(1)}, bf16[96,3840]{1,0:T(8,128)(2,1)S(1)}, u32[]{:S(2)}, u32[]{:S(2)}) collective-permute-start(bf16[96,3840]{1,0:T(8,128)(2,1)S(1)} %slice.358), channel_id=1, source_target_pairs={{0,4},{2,6},{4,0},{6,2},{8,12},{10,14},{12,8},{14,10},{16,20},{18,... | collective-permute-start | bytes 2211848 | tf_op jit(solution)/shard_map/ppermute | solution.py:764
  265.9 9.4 %collective-permute-start.27 = (bf16[192,768]{1,0:T(8,128)(2,1)S(1)}, bf16[192,768]{1,0:T(8,128)(2,1)S(1)}, u32[]{:S(2)}, u32[]{:S(2)}) collective-permute-start(bf16[192,768]{1,0:T(8,128)(2,1)S(1)} %slice.362), channel_id=1, source_target_pairs={{0,8},{2,10},{4,12},{6,14},{8,0},{10,2},{12,4},{14,6},{16,24},{18,... | collective-permute-start | bytes 884744 | tf_op jit(solution)/shard_map/ppermute | solution.py:764
  271.6 7.7 %collective-permute-start.22 = (bf16[48,3840]{1,0:T(8,128)(2,1)S(1)}, bf16[48,3840]{1,0:T(8,128)(2,1)S(1)}, u32[]{:S(2)}, u32[]{:S(2)}) collective-permute-start(bf16[48,3840]{1,0:T(8,128)(2,1)S(1)} %slice.361), channel_id=1, source_target_pairs={{0,8},{2,10},{4,12},{6,14},{8,0},{10,2},{12,4},{14,6},{16,24},{18,... | collective-permute-start | bytes 1105928 | tf_op jit(solution)/shard_map/ppermute | solution.py:764
  275.4 7.3 %collective-permute-start.28 = (bf16[96,768]{1,0:T(8,128)(2,1)S(1)}, bf16[96,768]{1,0:T(8,128)(2,1)S(1)}, u32[]{:S(2)}, u32[]{:S(2)}) collective-permute-start(bf16[96,768]{1,0:T(8,128)(2,1)S(1)} %slice.365), channel_id=1, source_target_pairs={{0,16},{2,18},{4,20},{6,22},{8,24},{10,26},{12,28},{14,30},{16,0},... | collective-permute-start | bytes 442376 | tf_op jit(solution)/shard_map/ppermute | solution.py:764
  279.3 9.9 %copy-start.1 = (bf16[768,768]{1,0:T(8,128)(2,1)S(1)}, bf16[768,768]{1,0:T(8,128)(2,1)}, u32[]{:S(2)}) copy-start(bf16[768,768]{1,0:T(8,128)(2,1)} %param.30) | copy-start | bytes 3538948
  279.4 8.5 %collective-permute-start.23 = (bf16[24,3840]{1,0:T(8,128)(2,1)S(1)}, bf16[24,3840]{1,0:T(8,128)(2,1)S(1)}, u32[]{:S(2)}, u32[]{:S(2)}) collective-permute-start(bf16[24,3840]{1,0:T(8,128)(2,1)S(1)} %slice.364), channel_id=1, source_target_pairs={{0,16},{2,18},{4,20},{6,22},{8,24},{10,26},{12,28},{14,30},{16,0},... | collective-permute-start | bytes 552968 | tf_op jit(solution)/shard_map/ppermute | solution.py:764
  (47 other events, 162.9 us)
